TPU v7x, 256 devices: a whole 4x4x8 slice. The times are simulated.
256 devices in a mesh: space: 8 (over x, core), spec: 32 (over z, y).
Axes of the slice: x: 4, y: 4, z: 8, core: 2. Of those that a mesh axis runs over, the one named last changes fastest.
Arguments:
- spectrum: float32 [32, 36, 512, 128], P('spec', None, 'space'), may hold values from 0.2 to 2
- sea_depth: float32 [512, 128], P('space'), may hold values from 5 to 200
- current: float32 [2, 512, 128], P(None, 'space'), may hold values from -3 to 3
- depth_slope: float32 [2, 512, 128], P(None, 'space'), may hold values from -2.5 to 2.5
- wind_forcing: float32 [512, 128], P('space'), may hold values from 0.2 to 2
- wind_angle: float32 [512, 128], P('space'), may hold values from -3.140625 to 3.140625
- land_sea: int32 [512, 128], P('space'), may hold values from 0 to 1, as said below
- quad_table: int32 [4, 1152], replicated, may hold values from 0 to 1151, as said below
- coupling: float32 [1152], replicated, may hold values from 0.01 to 0.04
Outputs:
- updated: float32 [32, 36, 512, 128], P('spec', None, 'space')
Inputs may be any that keep to these rules, and one draw needn't show every extreme that they name: `land_sea`: each tile of 64 grid rows holds at most 4096 sea cells; some tile holds exactly that many. `quad_table`: quadruplet partners of bin i * 36 + j: rows 0 and 2 lie 2 or 3 frequencies above i, rows 1 and 3 lie 2 or 3 below, clamped to the frequency range; in direction row 0 lies 1 or 2 bins above j, row 2 1 or 2 below, row 1 3 or 4 below, row 3 3 or 4 above, periodic.
All inputs are finite; a program needn't handle non-finite values.
Results may differ from a plain program's by a relative error of at most 0.0001.
Values sent between devices are 32-bit elements; how exact they have to be, the bound alone decides.
A program may use at most 64 MiB of HBM per device.

v0:
```python
import functools
import math

import jax
import jax.numpy as jnp
import numpy as np
from jax import lax
from jax.experimental import pallas as pl
from jax.experimental.pallas import tpu as pltpu
from jax.sharding import PartitionSpec as P

NFREQ, NDIR, ROWS, COLS = 32, 36, 64, 128
NY_DEV = 4
PACKED = 32
PAD = 4
WIDE = NDIR + 2 * PAD
F32 = jnp.float32
VMEM = pl.BlockSpec(memory_space=pltpu.VMEM)
SMEM = pl.BlockSpec(memory_space=pltpu.SMEM)
ROW_SIGN = (1, -1, 1, -1)
ROW_DIRS = ((1, 2), (-3, -4), (-1, -2), (3, 4))


def iota(shape, axis):
    return lax.broadcasted_iota(jnp.int32, shape, axis)


def sea_positions(land):
    wet = land.astype(jnp.bfloat16)
    before = (iota((COLS, COLS), 0) < iota((COLS, COLS), 1)).astype(F32).astype(jnp.bfloat16)
    rank = jnp.dot(wet, before, preferred_element_type=F32)
    count = jnp.dot(wet, jnp.ones((COLS, COLS), jnp.bfloat16), preferred_element_type=F32)
    above = (iota((ROWS, ROWS), 0) > iota((ROWS, ROWS), 1)).astype(F32).astype(jnp.bfloat16)
    start = jnp.dot(above, count.astype(jnp.bfloat16), preferred_element_type=F32)
    return start.astype(jnp.int32), rank.astype(jnp.int32), count.astype(jnp.int32)


def packing(land_ref, lane_ref, row_ref, ends_ref):
    land = land_ref[...]
    start, rank, count = sea_positions(land)
    lanes = iota((ROWS, COLS), 1)
    code = jnp.where(land > 0, lanes | ((lanes - rank) << 8), 0)
    for bit in range(7):
        moved = pltpu.roll(code, COLS - (1 << bit), 1)
        comes = ((moved >> (8 + bit)) & 1) == 1
        stays = ((code >> (8 + bit)) & 1) == 0
        code = jnp.where(comes, moved, jnp.where(stays, code, 0))
    lane_ref[...] = jnp.take_along_axis(code & 127, (lanes - start) & 127, axis=1)
    ends_ref[...] = start + count
    slots = iota((PACKED, COLS), 0) * COLS + iota((PACKED, COLS), 1)

    def count_row(r, total):
        return total + (ends_ref[pl.ds(r, 1), :] <= slots).astype(jnp.int32)

    row_ref[...] = lax.fori_loop(0, ROWS, count_row, jnp.zeros((PACKED, COLS), jnp.int32), unroll=8)


def pack(spectrum_ref, lane_ref, row_ref, packed_ref):
    def one(d, carry):
        staged = []
        for v in range(8):
            rows = slice(8 * v, 8 * v + 8)
            staged.append(jnp.take_along_axis(spectrum_ref[d, rows, :], lane_ref[rows, :], axis=1))
        for q in range(4):
            rows = slice(8 * q, 8 * q + 8)
            source = row_ref[rows, :]
            within, block = source & 7, source >> 3
            out = jnp.zeros((8, COLS), F32)
            for v in range(q, 8):
                out = jnp.where(block == v, jnp.take_along_axis(staged[v], within, axis=0), out)
            packed_ref[d, rows, :] = out
        return carry

    lax.fori_loop(0, NDIR, one, 0)


def unpacking(land_ref, slot_row_ref, slot_lane_ref):
    start, rank, _ = sea_positions(land_ref[...])
    lanes = iota((ROWS, COLS), 1)
    slot_row_ref[...] = (start + ((lanes - start) & 127)) >> 7
    slot_lane_ref[...] = (start + rank) & 127


def unpack_block(load, slot_row, slot_lane, v):
    within, block = slot_row & 7, slot_row >> 3
    staged = jnp.take_along_axis(load(0), within, axis=0)
    for q in range(1, min(v, 3) + 1):
        staged = jnp.where(block == q, jnp.take_along_axis(load(q), within, axis=0), staged)
    return jnp.take_along_axis(staged, slot_lane, axis=1)


def transport_fields(angular, root, depth_ref, current_ref, slope_ref, forcing_ref, angle_ref, fields):
    tanh_term = jnp.tanh(angular * angular / 9.81 * depth_ref[...])
    fields[0] = (0.025 * (9.81 / 2.0)) / angular * tanh_term
    fields[1] = 0.025 * current_ref[0]
    fields[2] = 0.025 * current_ref[1]
    turning = 0.2 * (1.0 - tanh_term)
    fields[3] = turning * slope_ref[0]
    fields[4] = turning * slope_ref[1]
    wind = 0.05 * root * forcing_ref[...]
    fields[5] = wind * jnp.cos(angle_ref[...])
    fields[6] = wind * jnp.sin(angle_ref[...])


def transport(trig_ref, spectrum_ref, land_ref, fields, base, ahead, behind, edges, lo, hi):
    rows, lanes = iota((ROWS, COLS), 0), iota((ROWS, COLS), 1)

    def one(j, carry):
        cosine, sine = trig_ref[j], trig_ref[NDIR + j]
        energy = jnp.where(land_ref[...] > 0, spectrum_ref[j], 0.0)
        group = fields[0]
        along = group * cosine + fields[1]
        fx, bx = jnp.maximum(along, 0.0) * energy, jnp.minimum(along, 0.0) * energy
        across = group * sine + fields[2]
        fy, by = jnp.maximum(across, 0.0) * energy, jnp.minimum(across, 0.0) * energy
        turn = sine * fields[3] - cosine * fields[4]
        ft, bt = jnp.maximum(turn, 0.0) * energy, jnp.minimum(turn, 0.0) * energy
        edges[0, pl.ds(j, 1), :] = fx[ROWS - 1 :, :]
        edges[1, pl.ds(j, 1), :] = bx[:1, :]
        prev_x = jnp.where(rows == 0, 0.0, pltpu.roll(fx, 1, 0))
        next_x = jnp.where(rows == ROWS - 1, 0.0, pltpu.roll(bx, ROWS - 1, 0))
        prev_y = jnp.where(lanes == 0, 0.0, pltpu.roll(fy, 1, 1))
        next_y = jnp.where(lanes == COLS - 1, 0.0, pltpu.roll(by, COLS - 1, 1))
        change = (fx + next_x - (prev_x + bx)) + (fy + next_y - (prev_y + by)) + (ft - bt)
        wind = jnp.maximum(cosine * fields[5] + sine * fields[6], 0.0) * energy
        base[j] = energy - change + wind
        ahead[j + 1] = ft
        behind[j] = bt
        return carry

    lax.fori_loop(lo, hi, one, 0)


def quadruplets(table_ref, coupling_ref, decay_ref, x, square, q_one, q_two, n):
    def one(j, carry):
        for f in range(NY_DEV):
            k = f * NDIR + j
            energy = x[(3 + f) * NDIR + j]
            a, b = x[table_ref[k]], x[table_ref[144 + k]]
            c, d = x[table_ref[288 + k]], x[table_ref[432 + k]]
            scaled = coupling_ref[k] * energy
            first = scaled * (energy * (a + b) - 2.0 * a * b)
            second = scaled * (energy * (c + d) - 2.0 * c * d)
            q_one[f, PAD + j] = first
            q_two[f, PAD + j] = second
            n[3 + f, j] = -2.0 * (first + second) - (decay_ref[f] * square) * energy
        return carry

    lax.fori_loop(0, NDIR, one, 0)
    for f in range(NY_DEV):
        for q in (q_one, q_two):
            for i in range(PAD):
                q[f, i] = q[f, NDIR + i]
                q[f, PAD + NDIR + i] = q[f, PAD + i]


def scatter_target(mask_ref, q_one, q_two, t, j, total):
    for row in range(4):
        q = q_one if row < 2 else q_two
        for step in range(2):
            f = t - 3 - ROW_SIGN[row] * (2 + step)
            if not 0 <= f < NY_DEV:
                continue
            for which in range(2):
                source = j - ROW_DIRS[row][which] + PAD
                at = (((row * 2 + step) * 2 + which) * NY_DEV + f) * WIDE
                term = mask_ref[at + source] * q[f, source]
                total = term if total is None else total + term
    return total


def pack_kernel(spectrum_ref, land_ref, packed_ref, lane_ref, row_ref, ends_ref):
    packing(land_ref, lane_ref, row_ref, ends_ref)
    pack(spectrum_ref, lane_ref, row_ref, packed_ref)


def quad_kernel(table_ref, mask_ref, coupling_ref, decay_ref, x_ref, square_ref, n_ref, q_one, q_two):
    quadruplets(table_ref, coupling_ref, decay_ref, x_ref, square_ref[...], q_one, q_two, n_ref)

    def one(j, carry):
        for t in range(10):
            own = n_ref[t, j] if 3 <= t < 7 else None
            n_ref[t, j] = scatter_target(mask_ref, q_one, q_two, t, j, own)
        return carry

    lax.fori_loop(0, NDIR, one, 0)


def final_kernel(
    scalars_ref, trig_ref, spectrum_ref, depth_ref, current_ref, slope_ref, forcing_ref, angle_ref, land_ref,
    preceding_ref, following_ref, source_ref, out_ref, fields, base, ahead, behind, edges, slot_row, slot_lane,
):
    transport_fields(scalars_ref[0], scalars_ref[1], depth_ref, current_ref, slope_ref, forcing_ref, angle_ref, fields)
    transport(trig_ref, spectrum_ref, land_ref, fields, base, ahead, behind, edges, 0, NDIR)
    ahead[0] = ahead[NDIR]
    behind[NDIR] = behind[0]
    unpacking(land_ref, slot_row, slot_lane)

    def one(j, carry):
        base[j, 0:1, :] += preceding_ref[pl.ds(j, 1), :]
        base[j, ROWS - 1 :, :] -= following_ref[pl.ds(j, 1), :]
        for v in range(8):
            rows = slice(8 * v, 8 * v + 8)
            source = unpack_block(
                lambda q: source_ref[j, 8 * q : 8 * q + 8, :], slot_row[rows, :], slot_lane[rows, :], v
            )
            moved = base[j, rows, :] + ahead[j, rows, :] - behind[j + 1, rows, :]
            out_ref[j, rows, :] = jnp.where(land_ref[rows, :] > 0, moved + source, 0.0)
        return carry

    lax.fori_loop(0, NDIR, one, 0)


def edge_kernel(scalars_ref, trig_ref, spectrum_ref, depth_ref, current_ref, land_ref, edges_ref):
    for side, row in ((0, ROWS - 1), (1, 0)):
        at = slice(row, row + 1)
        angular = scalars_ref[0]
        group = (0.025 * (9.81 / 2.0)) / angular * jnp.tanh(angular * angular / 9.81 * depth_ref[at, :])
        flow = 0.025 * current_ref[0, at, :]
        wet = land_ref[at, :] > 0

        def one(j, carry):
            energy = jnp.where(wet, spectrum_ref[j, at, :], 0.0)
            along = group * trig_ref[j] + flow
            edge = jnp.maximum(along, 0.0) if side == 0 else jnp.minimum(along, 0.0)
            edges_ref[side, pl.ds(j, 1), :] = edge * energy
            return carry

        lax.fori_loop(0, NDIR, one, 0)


def quad_masks(block, z):
    table = block.reshape(4, NY_DEV, NDIR)
    table = jnp.concatenate([table[..., -PAD:], table, table[..., :PAD]], axis=-1)
    freq = z * NY_DEV + jnp.arange(NY_DEV)
    direction = (jnp.arange(WIDE) - PAD) % NDIR
    masks = []
    for row in range(4):
        near = jnp.clip(freq + 2 * ROW_SIGN[row], 0, NFREQ - 1)
        far = jnp.clip(freq + 3 * ROW_SIGN[row], 0, NFREQ - 1)
        for target in (near, jnp.where(far == near, -NFREQ, far)):
            for turn in ROW_DIRS[row]:
                bins = target[:, None] * NDIR + ((direction + turn) % NDIR)[None, :]
                masks.append(table[row] == bins)
    return jnp.stack(masks).astype(F32).reshape(-1)


def on_device(spectrum, sea_depth, current, depth_slope, wind_forcing, wind_angle, land_sea, quad_table, coupling):
    spectrum = spectrum.reshape(NDIR, ROWS, COLS)
    index = lax.axis_index("spec")
    z, y = index // NY_DEV, index % NY_DEV
    planes = NFREQ // NY_DEV
    heading = np.float32(2.0 * np.pi / NDIR) * np.arange(NDIR, dtype=np.float32)
    trig = jnp.asarray(np.concatenate([np.cos(heading), np.sin(heading)]).astype(np.float32))
    growth = jnp.power(1.1, index.astype(F32))
    scalars = jnp.stack([2.0 * jnp.pi * 0.04 * growth, jnp.sqrt(growth)])
    own = z * NY_DEV + jnp.arange(NY_DEV)
    decay = 0.3 * jnp.power(1.1, (own - (NFREQ - 1)).astype(F32)) ** 2

    packed = pl.pallas_call(
        pack_kernel,
        out_shape=jax.ShapeDtypeStruct((NDIR, PACKED, COLS), F32),
        in_specs=[VMEM, VMEM],
        out_specs=VMEM,
        scratch_shapes=[
            pltpu.VMEM((ROWS, COLS), jnp.int32),
            pltpu.VMEM((PACKED, COLS), jnp.int32),
            pltpu.VMEM((ROWS, COLS), jnp.int32),
        ],
        compiler_params=pltpu.CompilerParams(vmem_limit_bytes=32 << 20),
    )(spectrum, land_sea)

    edges = pl.pallas_call(
        edge_kernel,
        out_shape=jax.ShapeDtypeStruct((2, NDIR, COLS), F32),
        in_specs=[SMEM, SMEM] + [VMEM] * 4,
        out_specs=VMEM,
    )(scalars, trig, spectrum, sea_depth, current, land_sea)
    spaces = lax.axis_size("space")
    preceding = lax.ppermute(edges[0], "space", [(i, i + 1) for i in range(spaces - 1)])
    following = lax.ppermute(edges[1], "space", [(i + 1, i) for i in range(spaces - 1)])

    groups = [[a * NY_DEV + b for b in range(NY_DEV)] for a in range(planes)]
    columns = [[a * NY_DEV + b for a in range(planes)] for b in range(NY_DEV)]
    quarter = packed.reshape(NDIR, NY_DEV, 8, COLS).swapaxes(0, 1)
    plane = lax.all_to_all(quarter, "spec", 0, 0, axis_index_groups=groups, tiled=True)
    up = [(i, i + NY_DEV) for i in range(NFREQ - NY_DEV)]
    down = [(i + NY_DEV, i) for i in range(NFREQ - NY_DEV)]
    below = lax.ppermute(plane[1:], "spec", up)
    above = lax.ppermute(plane[:-1], "spec", down)
    total = lax.psum(plane.sum(axis=(0, 1)), "spec", axis_index_groups=columns)
    mean = total / (NFREQ * NDIR)
    x = jnp.concatenate([below, plane, above], axis=0).reshape(10 * NDIR, 8, COLS)
    block = lax.dynamic_slice(quad_table, (0, z * 144), (4, 144))
    table = (block - (z * NY_DEV - 3) * NDIR).reshape(-1)
    n = pl.pallas_call(
        quad_kernel,
        out_shape=jax.ShapeDtypeStruct((10, NDIR, 8, COLS), F32),
        in_specs=[SMEM] * 4 + [VMEM] * 2,
        out_specs=VMEM,
        scratch_shapes=[pltpu.VMEM((NY_DEV, WIDE, 8, COLS), F32)] * 2,
        compiler_params=pltpu.CompilerParams(vmem_limit_bytes=32 << 20),
    )(table, quad_masks(block, z), lax.dynamic_slice(coupling, (z * 144,), (144,)), decay, x, mean * mean)
    from_below = lax.ppermute(n[7:], "spec", up)
    from_above = lax.ppermute(n[:3], "spec", down)
    first = jnp.where(z == 0, n[:3].sum(axis=0), 0.0)
    last = jnp.where(z == planes - 1, n[7:].sum(axis=0), 0.0)
    source = n[3:7] + jnp.concatenate([from_below, last[None]]) + jnp.concatenate([first[None], from_above])
    source = lax.all_to_all(source, "spec", 0, 0, axis_index_groups=groups, tiled=True)
    source = source.swapaxes(0, 1).reshape(NDIR, PACKED, COLS)

    big = pltpu.VMEM((NDIR, ROWS, COLS), F32)
    longer = pltpu.VMEM((NDIR + 1, ROWS, COLS), F32)
    tile = pltpu.VMEM((ROWS, COLS), jnp.int32)
    out = pl.pallas_call(
        final_kernel,
        out_shape=jax.ShapeDtypeStruct((NDIR, ROWS, COLS), F32),
        in_specs=[SMEM, SMEM] + [VMEM] * 10,
        out_specs=VMEM,
        scratch_shapes=[
            pltpu.VMEM((7, ROWS, COLS), F32), big, longer, longer, pltpu.VMEM((2, NDIR, COLS), F32), tile, tile
        ],
        compiler_params=pltpu.CompilerParams(vmem_limit_bytes=40 << 20),
    )(scalars, trig, spectrum, sea_depth, current, depth_slope, wind_forcing, wind_angle, land_sea, preceding, following, source)
    return out.reshape(1, NDIR, ROWS, COLS)


def solution(mesh):
    return jax.shard_map(
        on_device,
        mesh=mesh,
        in_specs=(
            P("spec", None, "space", None),
            P("space", None),
            P(None, "space", None),
            P(None, "space", None),
            P("space", None),
            P("space", None),
            P("space", None),
            P(),
            P(),
        ),
        out_specs=P("spec", None, "space", None),
        check_vma=False,
    )
```

profile of v0, /device:TPU:107, one launch (start us, length us, event | category | flops | bytes accessed | tf_op | source)
XLA Modules:
  0.0 95.5 jit_solution(11923796676857736747)
XLA Ops:
  0.0 1.3 %copy-done = f32[1,36,64,128]{3,2,1,0:T(8,128)S(1)} copy-done((f32[1,36,64,128]{3,2,1,0:T(8,128)S(1)}, f32[1,36,64,128]{3,2,1,0:T(8,128)}, u32[]{:S(2)}) %copy-start) | copy-done | bytes 1179672
  1.3 0.8 copy-done.2
  2.0 4.1 %shard_map.101 = f32[36,32,128]{2,1,0:T(8,128)S(1)} custom-call(f32[36,64,128]{2,1,0:T(8,128)S(1)} %bitcast.24, s32[64,128]{1,0:T(8,128)S(1)} %copy-done.2), custom_call_target="tpu_custom_call" | custom-call | tf_op jit(solution)/shard_map/pallas_call | solution.py:260
  6.1 0.9 copy_bitcast_fusion.1
  7.0 4.3 %all-to-all-start = ((f32[4,36,8,128]{3,2,1,0:T(8,128)}), f32[4,36,8,128]{3,2,1,0:T(8,128)S(1)}, u32[]{:S(2)}, u32[]{:S(2)}) async-start(f32[4,36,8,128]{3,2,1,0:T(8,128)} %copy_bitcast_fusion.1), calls=%async_computation | async-start | bytes 1179648 | tf_op jit(solution)/shard_map/all_to_all | solution.py:286
  11.6 0.8 broadcast_subtract_fusion
  13.8 5.6 %all-to-all-done = f32[4,36,8,128]{3,2,1,0:T(8,128)S(1)} async-done(((f32[4,36,8,128]{3,2,1,0:T(8,128)}), f32[4,36,8,128]{3,2,1,0:T(8,128)S(1)}, u32[]{:S(2)}, u32[]{:S(2)}) %all-to-all-start) | async-done | bytes 589856 | tf_op jit(solution)/shard_map/all_to_all | solution.py:286
  19.5 4.8 %collective-permute-start.2 = (f32[3,36,8,128]{3,2,1,0:T(8,128)S(1)}, f32[3,36,8,128]{3,2,1,0:T(8,128)S(1)}, u32[]{:S(2)}, u32[]{:S(2)}) collective-permute-start(f32[3,36,8,128]{3,2,1,0:T(8,128)S(1)} %get-tuple-element.11), channel_id=1, source_target_pairs={{0,4},{1,5},{2,6},{3,7},{4,8},{5,9},{6,10},{7,11},{8,12},{9,13},{1... | collective-permute-start | bytes 1327112 | tf_op jit(solution)/shard_map/ppermute | solution.py:289
  24.3 1.9 %collective-permute-start.3 = (f32[3,36,8,128]{3,2,1,0:T(8,128)S(1)}, f32[3,36,8,128]{3,2,1,0:T(8,128)S(1)}, u32[]{:S(2)}, u32[]{:S(2)}) collective-permute-start(f32[3,36,8,128]{3,2,1,0:T(8,128)S(1)} %get-tuple-element.12), channel_id=1, source_target_pairs={{4,0},{5,1},{6,2},{7,3},{8,4},{9,5},{10,6},{11,7},{12,8},{13,9},{1... | collective-permute-start | bytes 1327112 | tf_op jit(solution)/shard_map/ppermute | solution.py:290
  26.5 0.8 dynamic_slice.7.coupling_ref
  27.4 15.0 %psum.7 = f32[8,128]{1,0:T(8,128)S(1)} all-reduce(f32[8,128]{1,0:T(8,128)S(1)} %reduce_sum.27), channel_id=1, replica_groups={{0,4,8,12,16,20,24,28},{1,5,9,13,17,21,25,29},{2,6,10,14,18,22,26,30},{..., use_global_device_ids=true, to_apply=%region_1.2 | all-reduce | flops 1024 | bytes 8192 | tf_op jit(solution)/shard_map/psum | solution.py:291
  42.6 3.4 %shard_map.102 = f32[10,36,8,128]{3,2,1,0:T(8,128)S(1)} custom-call(s32[576]{0:T(1024)S(1)} %reshape.844.table_ref, f32[2816]{0:T(1024)S(1)} %reshape.850.mask_ref, f32[144]{0:T(256)S(1)} %dynamic_slice.7.coupling_ref, f32[4]{0:T(128)S(1)} %multiply_multiply_fusion.1.decay_ref, f32[360,8,128]{2,1,0:T(8,128)S(1)} %bitcast.26, ...), custom_call_target="tpu_custom_call" | custom-call | tf_op jit(solution)/shard_map/pallas_call | solution.py:296
  46.1 5.1 %collective-permute-start.4 = (f32[3,36,8,128]{3,2,1,0:T(8,128)S(1)}, f32[3,36,8,128]{3,2,1,0:T(8,128)S(1)}, u32[]{:S(2)}, u32[]{:S(2)}) collective-permute-start(f32[3,36,8,128]{3,2,1,0:T(8,128)S(1)} %get-tuple-element.10), channel_id=1, source_target_pairs={{0,4},{1,5},{2,6},{3,7},{4,8},{5,9},{6,10},{7,11},{8,12},{9,13},{1... | collective-permute-start | bytes 1327112 | tf_op jit(solution)/shard_map/ppermute | solution.py:304
  51.2 1.9 %collective-permute-start.5 = (f32[3,36,8,128]{3,2,1,0:T(8,128)S(1)}, f32[3,36,8,128]{3,2,1,0:T(8,128)S(1)}, u32[]{:S(2)}, u32[]{:S(2)}) collective-permute-start(f32[3,36,8,128]{3,2,1,0:T(8,128)S(1)} %get-tuple-element.9), channel_id=1, source_target_pairs={{4,0},{5,1},{6,2},{7,3},{8,4},{9,5},{10,6},{11,7},{12,8},{13,9},{1... | collective-permute-start | bytes 1327112 | tf_op jit(solution)/shard_map/ppermute | solution.py:305
  53.2 3.3 %collective-permute-done.4 = f32[3,36,8,128]{3,2,1,0:T(8,128)S(1)} collective-permute-done((f32[3,36,8,128]{3,2,1,0:T(8,128)S(1)}, f32[3,36,8,128]{3,2,1,0:T(8,128)S(1)}, u32[]{:S(2)}, u32[]{:S(2)}) %collective-permute-start.4) | collective-permute-done | bytes 442400 | tf_op jit(solution)/shard_map/ppermute | solution.py:304
  56.4 5.0 %collective-permute-done.5 = f32[3,36,8,128]{3,2,1,0:T(8,128)S(1)} collective-permute-done((f32[3,36,8,128]{3,2,1,0:T(8,128)S(1)}, f32[3,36,8,128]{3,2,1,0:T(8,128)S(1)}, u32[]{:S(2)}, u32[]{:S(2)}) %collective-permute-start.5) | collective-permute-done | bytes 442400 | tf_op jit(solution)/shard_map/ppermute | solution.py:305
  61.5 0.9 fusion
  62.4 4.6 %all-to-all-start.1 = ((f32[4,36,8,128]{3,2,1,0:T(8,128)}), f32[4,36,8,128]{3,2,1,0:T(8,128)S(1)}, u32[]{:S(2)}, u32[]{:S(2)}) async-start(f32[4,36,8,128]{3,2,1,0:T(8,128)} %fusion), calls=%async_computation.1 | async-start | bytes 1179648 | tf_op jit(solution)/shard_map/all_to_all | solution.py:309
  67.8 2.6 %shard_map.100 = f32[2,36,128]{2,1,0:T(8,128)} custom-call(f32[2]{0:T(128)} %pad_maximum_fusion.1.scalars_ref, f32[72]{0:T(128)} %constant.127.clone.trig_ref, f32[36,64,128]{2,1,0:T(8,128)} %bitcast.23, f32[64,128]{1,0:T(8,128)} %depth_ref.3, f32[2,64,128]{2,1,0:T(8,128)} %current_ref.3, s32[64,128]{1,0:T(8,128)} %land_ref.5), custom_call_target="tpu_custom_call" | custom-call | tf_op jit(solution)/shard_map/pallas_call | solution.py:273
  70.4 0.7 slice_bitcast_fusion
  71.2 10.1 %collective-permute-start = (f32[36,128]{1,0:T(8,128)S(1)}, f32[36,128]{1,0:T(8,128)S(1)}, u32[]{:S(2)}, u32[]{:S(2)}) collective-permute-start(f32[36,128]{1,0:T(8,128)S(1)} %get-tuple-element.14), channel_id=1, source_target_pairs={{0,32},{32,64},{64,96},{96,128},{128,160},{160,192},{192,224},{1,3... | collective-permute-start | bytes 55304 | tf_op jit(solution)/shard_map/ppermute | solution.py:280
  81.3 1.9 %collective-permute-start.1 = (f32[36,128]{1,0:T(8,128)S(1)}, f32[36,128]{1,0:T(8,128)S(1)}, u32[]{:S(2)}, u32[]{:S(2)}) collective-permute-start(f32[36,128]{1,0:T(8,128)S(1)} %get-tuple-element.13), channel_id=1, source_target_pairs={{32,0},{64,32},{96,64},{128,96},{160,128},{192,160},{224,192},{33,... | collective-permute-start | bytes 55304 | tf_op jit(solution)/shard_map/ppermute | solution.py:281
  83.3 3.1 %collective-permute-done.1.following_ref = f32[36,128]{1,0:T(8,128)S(1)} collective-permute-done((f32[36,128]{1,0:T(8,128)S(1)}, f32[36,128]{1,0:T(8,128)S(1)}, u32[]{:S(2)}, u32[]{:S(2)}) %collective-permute-start.1) | collective-permute-done | bytes 18464 | tf_op jit(solution)/shard_map/ppermute | solution.py:281
  86.4 9.1 %shard_map.103 = f32[36,64,128]{2,1,0:T(8,128)} custom-call(f32[2]{0:T(128)S(1)} %copy-done.10, f32[72]{0:T(128)S(1)} %copy-done.9, f32[36,64,128]{2,1,0:T(8,128)S(1)} %bitcast.25, f32[64,128]{1,0:T(8,128)S(1)} %copy-done.5, f32[2,64,128]{2,1,0:T(8,128)S(1)} %copy-done.4, f32[2,64,128]{2,1,0:T(8,128)S(1)} %copy-done.6, f32[64,128]{1,0:T(8,128)S(1)} %copy-done.7, ...), custom_call_target="tpu_custom_call" | custom-call | tf_op jit(solution)/shard_map/pallas_call | solution.py:315
  (66 shorter events, 3.1 us)
Async XLA Ops:
  0.0 1.3 %copy-start = (f32[1,36,64,128]{3,2,1,0:T(8,128)S(1)}, f32[1,36,64,128]{3,2,1,0:T(8,128)}, u32[]{:S(2)}) copy-start(f32[1,36,64,128]{3,2,1,0:T(8,128)} %param.10) | copy-start | bytes 3538948
  1.3 0.8 copy-start.2
  7.0 12.4 %all-to-all-start = ((f32[4,36,8,128]{3,2,1,0:T(8,128)}), f32[4,36,8,128]{3,2,1,0:T(8,128)S(1)}, u32[]{:S(2)}, u32[]{:S(2)}) async-start(f32[4,36,8,128]{3,2,1,0:T(8,128)} %copy_bitcast_fusion.1), calls=%async_computation | async-start | bytes 1179648 | tf_op jit(solution)/shard_map/all_to_all | solution.py:286
  19.5 23.0 %collective-permute-start.2 = (f32[3,36,8,128]{3,2,1,0:T(8,128)S(1)}, f32[3,36,8,128]{3,2,1,0:T(8,128)S(1)}, u32[]{:S(2)}, u32[]{:S(2)}) collective-permute-start(f32[3,36,8,128]{3,2,1,0:T(8,128)S(1)} %get-tuple-element.11), channel_id=1, source_target_pairs={{0,4},{1,5},{2,6},{3,7},{4,8},{5,9},{6,10},{7,11},{8,12},{9,13},{1... | collective-permute-start | bytes 1327112 | tf_op jit(solution)/shard_map/ppermute | solution.py:289
  24.3 18.2 %collective-permute-start.3 = (f32[3,36,8,128]{3,2,1,0:T(8,128)S(1)}, f32[3,36,8,128]{3,2,1,0:T(8,128)S(1)}, u32[]{:S(2)}, u32[]{:S(2)}) collective-permute-start(f32[3,36,8,128]{3,2,1,0:T(8,128)S(1)} %get-tuple-element.12), channel_id=1, source_target_pairs={{4,0},{5,1},{6,2},{7,3},{8,4},{9,5},{10,6},{11,7},{12,8},{13,9},{1... | collective-permute-start | bytes 1327112 | tf_op jit(solution)/shard_map/ppermute | solution.py:290
  46.1 10.4 %collective-permute-start.4 = (f32[3,36,8,128]{3,2,1,0:T(8,128)S(1)}, f32[3,36,8,128]{3,2,1,0:T(8,128)S(1)}, u32[]{:S(2)}, u32[]{:S(2)}) collective-permute-start(f32[3,36,8,128]{3,2,1,0:T(8,128)S(1)} %get-tuple-element.10), channel_id=1, source_target_pairs={{0,4},{1,5},{2,6},{3,7},{4,8},{5,9},{6,10},{7,11},{8,12},{9,13},{1... | collective-permute-start | bytes 1327112 | tf_op jit(solution)/shard_map/ppermute | solution.py:304
  51.2 10.3 %collective-permute-start.5 = (f32[3,36,8,128]{3,2,1,0:T(8,128)S(1)}, f32[3,36,8,128]{3,2,1,0:T(8,128)S(1)}, u32[]{:S(2)}, u32[]{:S(2)}) collective-permute-start(f32[3,36,8,128]{3,2,1,0:T(8,128)S(1)} %get-tuple-element.9), channel_id=1, source_target_pairs={{4,0},{5,1},{6,2},{7,3},{8,4},{9,5},{10,6},{11,7},{12,8},{13,9},{1... | collective-permute-start | bytes 1327112 | tf_op jit(solution)/shard_map/ppermute | solution.py:305
  62.4 20.8 %all-to-all-start.1 = ((f32[4,36,8,128]{3,2,1,0:T(8,128)}), f32[4,36,8,128]{3,2,1,0:T(8,128)S(1)}, u32[]{:S(2)}, u32[]{:S(2)}) async-start(f32[4,36,8,128]{3,2,1,0:T(8,128)} %fusion), calls=%async_computation.1 | async-start | bytes 1179648 | tf_op jit(solution)/shard_map/all_to_all | solution.py:309
  67.0 19.4 %copy-start.1 = (f32[1,36,64,128]{3,2,1,0:T(8,128)S(1)}, f32[1,36,64,128]{3,2,1,0:T(8,128)}, u32[]{:S(2)}) copy-start(f32[1,36,64,128]{3,2,1,0:T(8,128)} %param.10) | copy-start | bytes 3538948
  67.0 19.4 %copy-start.3 = (s32[64,128]{1,0:T(8,128)S(1)}, s32[64,128]{1,0:T(8,128)}, u32[]{:S(2)}) copy-start(s32[64,128]{1,0:T(8,128)} %land_ref.5) | copy-start | bytes 98308
  67.0 19.4 %copy-start.4 = (f32[2,64,128]{2,1,0:T(8,128)S(1)}, f32[2,64,128]{2,1,0:T(8,128)}, u32[]{:S(2)}) copy-start(f32[2,64,128]{2,1,0:T(8,128)} %current_ref.3) | copy-start | bytes 196612
  67.0 19.4 %copy-start.5 = (f32[64,128]{1,0:T(8,128)S(1)}, f32[64,128]{1,0:T(8,128)}, u32[]{:S(2)}) copy-start(f32[64,128]{1,0:T(8,128)} %depth_ref.3) | copy-start | bytes 98308
  67.0 19.4 %copy-start.6 = (f32[2,64,128]{2,1,0:T(8,128)S(1)}, f32[2,64,128]{2,1,0:T(8,128)}, u32[]{:S(2)}) copy-start(f32[2,64,128]{2,1,0:T(8,128)} %slope_ref.1) | copy-start | bytes 196612
  67.0 19.4 %copy-start.7 = (f32[64,128]{1,0:T(8,128)S(1)}, f32[64,128]{1,0:T(8,128)}, u32[]{:S(2)}) copy-start(f32[64,128]{1,0:T(8,128)} %forcing_ref.1) | copy-start | bytes 98308
  67.0 19.4 %copy-start.8 = (f32[64,128]{1,0:T(8,128)S(1)}, f32[64,128]{1,0:T(8,128)}, u32[]{:S(2)}) copy-start(f32[64,128]{1,0:T(8,128)} %angle_ref.1) | copy-start | bytes 98308
  67.0 19.4 %copy-start.9 = (f32[72]{0:T(128)S(1)}, f32[72]{0:T(128)}, u32[]{:S(2)}) copy-start(f32[72]{0:T(128)} %constant.127.clone.trig_ref) | copy-start | bytes 868
  67.8 18.6 %copy-start.10 = (f32[2]{0:T(128)S(1)}, f32[2]{0:T(128)}, u32[]{:S(2)}) copy-start(f32[2]{0:T(128)} %pad_maximum_fusion.1.scalars_ref) | copy-start | bytes 28
  71.2 12.1 %collective-permute-start = (f32[36,128]{1,0:T(8,128)S(1)}, f32[36,128]{1,0:T(8,128)S(1)}, u32[]{:S(2)}, u32[]{:S(2)}) collective-permute-start(f32[36,128]{1,0:T(8,128)S(1)} %get-tuple-element.14), channel_id=1, source_target_pairs={{0,32},{32,64},{64,96},{96,128},{128,160},{160,192},{192,224},{1,3... | collective-permute-start | bytes 55304 | tf_op jit(solution)/shard_map/ppermute | solution.py:280
  81.3 5.1 %collective-permute-start.1 = (f32[36,128]{1,0:T(8,128)S(1)}, f32[36,128]{1,0:T(8,128)S(1)}, u32[]{:S(2)}, u32[]{:S(2)}) collective-permute-start(f32[36,128]{1,0:T(8,128)S(1)} %get-tuple-element.13), channel_id=1, source_target_pairs={{32,0},{64,32},{96,64},{128,96},{160,128},{192,160},{224,192},{33,... | collective-permute-start | bytes 55304 | tf_op jit(solution)/shard_map/ppermute | solution.py:281
where the time goes:
time: 96.1 us; the launch traced here: 95.5 us
  starting transfers between devices  34.7 us (36%)
  Pallas kernels  19.1 us (20%)
  waiting for transfers between devices  17 us (18%)
  blocking collectives  15 us (16%)
  local copies, waits for them, and re-layouts  4.91 us (5%)
  other arithmetic  4.29 us (4%)
    psum x1, blocking collectives, on_device(): total = lax.psum(plane.sum(axis=(0, 1)), 'spec', axis_index_groups=columns)  15 us
    ppermute x1, starting transfers between devices, on_device(): lax.ppermute(edges[0], 'space', [(i, i + 1) for i in range(spaces - 1)])  10.1 us
    pallas_call x1, Pallas kernels, on_device(): pl.pallas_call(final_kernel, out_shape=jax.ShapeDtypeStruct((NDIR, ROWS,...  9.06 us
    all_to_all x1, waiting for transfers between devices, on_device(): lax.all_to_all(quarter, 'spec', 0, 0, axis_index_groups=groups, tiled=True)  5.63 us
    ppermute x1, starting transfers between devices, on_device(): from_below = lax.ppermute(n[7:], 'spec', up)  5.14 us
    ppermute x1, waiting for transfers between devices, on_device(): from_above = lax.ppermute(n[:3], 'spec', down)  5.03 us
    ppermute x1, starting transfers between devices, on_device(): below = lax.ppermute(plane[1:], 'spec', up)  4.76 us
    all_to_all x1, starting transfers between devices, on_device(): lax.all_to_all(source, 'spec', 0, 0, axis_index_groups=groups, tiled=True)  4.63 us
  transfers between devices with their start and end apart: 8, of which 4 were waited for; matrix products, arithmetic and copies ran while one was open for 5% of the time, Pallas kernels for 3%

commit v1 on v0

v1 whole, which is shorter than its diff:
```python
import jax
import jax.numpy as jnp
import numpy as np
from jax import lax
from jax.experimental import pallas as pl
from jax.experimental.pallas import tpu as pltpu
from jax.sharding import PartitionSpec as P

NFREQ, NDIR, ROWS, COLS = 32, 36, 64, 128
NY_DEV = 4
PACKED = 32
PLANES = NFREQ // NY_DEV
HALO = 3
NCH = 3
PART = NDIR // NCH
PLANE_BINS = NY_DEV * NDIR
F32 = jnp.float32
VMEM = pl.BlockSpec(memory_space=pltpu.VMEM)
SMEM = pl.BlockSpec(memory_space=pltpu.SMEM)
ROW_SIGN = (1, -1, 1, -1)
ROW_DIRS = ((1, 2), (-3, -4), (-1, -2), (3, 4))


def iota(shape, axis):
    return lax.broadcasted_iota(jnp.int32, shape, axis)


def sea_positions(land):
    wet = land.astype(jnp.bfloat16)
    before = (iota((COLS, COLS), 0) < iota((COLS, COLS), 1)).astype(F32).astype(jnp.bfloat16)
    rank = jnp.dot(wet, before, preferred_element_type=F32)
    count = jnp.dot(wet, jnp.ones((COLS, COLS), jnp.bfloat16), preferred_element_type=F32)
    above = (iota((ROWS, ROWS), 0) > iota((ROWS, ROWS), 1)).astype(F32).astype(jnp.bfloat16)
    start = jnp.dot(above, count.astype(jnp.bfloat16), preferred_element_type=F32)
    return start.astype(jnp.int32), rank.astype(jnp.int32), count.astype(jnp.int32)


def packing(land_ref, lane_ref, row_ref, ends_ref):
    land = land_ref[...]
    start, rank, count = sea_positions(land)
    lanes = iota((ROWS, COLS), 1)
    code = jnp.where(land > 0, lanes | ((lanes - rank) << 8), 0)
    for bit in range(7):
        moved = pltpu.roll(code, COLS - (1 << bit), 1)
        comes = ((moved >> (8 + bit)) & 1) == 1
        stays = ((code >> (8 + bit)) & 1) == 0
        code = jnp.where(comes, moved, jnp.where(stays, code, 0))
    lane_ref[...] = jnp.take_along_axis(code & 127, (lanes - start) & 127, axis=1)
    ends_ref[...] = start + count
    slots = iota((PACKED, COLS), 0) * COLS + iota((PACKED, COLS), 1)

    def count_row(r, total):
        return total + (ends_ref[pl.ds(r, 1), :] <= slots).astype(jnp.int32)

    row_ref[...] = lax.fori_loop(0, ROWS, count_row, jnp.zeros((PACKED, COLS), jnp.int32), unroll=8)


def pack(spectrum_ref, lane_ref, row_ref, packed_ref, lo, hi):
    def one(d, carry):
        staged = []
        for v in range(8):
            rows = slice(8 * v, 8 * v + 8)
            staged.append(jnp.take_along_axis(spectrum_ref[d, rows, :], lane_ref[rows, :], axis=1))
        for q in range(4):
            rows = slice(8 * q, 8 * q + 8)
            source = row_ref[rows, :]
            within, block = source & 7, source >> 3
            out = jnp.zeros((8, COLS), F32)
            for v in range(q, 8):
                out = jnp.where(block == v, jnp.take_along_axis(staged[v], within, axis=0), out)
            packed_ref[d, rows, :] = out
        return carry

    lax.fori_loop(lo, hi, one, 0)


def unpacking(land_ref, slot_row_ref, slot_lane_ref):
    start, rank, _ = sea_positions(land_ref[...])
    lanes = iota((ROWS, COLS), 1)
    slot_row_ref[...] = (start + ((lanes - start) & 127)) >> 7
    slot_lane_ref[...] = (start + rank) & 127


def unpack_block(load, slot_row, slot_lane, v):
    within, block = slot_row & 7, slot_row >> 3
    staged = jnp.take_along_axis(load(0), within, axis=0)
    for q in range(1, min(v, 3) + 1):
        staged = jnp.where(block == q, jnp.take_along_axis(load(q), within, axis=0), staged)
    return jnp.take_along_axis(staged, slot_lane, axis=1)


def transport_fields(angular, root, depth_ref, current_ref, slope_ref, forcing_ref, angle_ref, fields):
    tanh_term = jnp.tanh(angular * angular / 9.81 * depth_ref[...])
    fields[0] = (0.025 * (9.81 / 2.0)) / angular * tanh_term
    fields[1] = 0.025 * current_ref[0]
    fields[2] = 0.025 * current_ref[1]
    turning = 0.2 * (1.0 - tanh_term)
    fields[3] = turning * slope_ref[0]
    fields[4] = turning * slope_ref[1]
    wind = 0.05 * root * forcing_ref[...]
    fields[5] = wind * jnp.cos(angle_ref[...])
    fields[6] = wind * jnp.sin(angle_ref[...])


def transport(trig_ref, spectrum_ref, land_ref, fields, base, ahead, behind, edges, lo, hi, beside):
    rows, lanes = iota((ROWS, COLS), 0), iota((ROWS, COLS), 1)

    def one(j, carry):
        cosine, sine = trig_ref[j], trig_ref[NDIR + j]
        energy = jnp.where(land_ref[...] > 0, spectrum_ref[j], 0.0)
        group = fields[0]
        along = group * cosine + fields[1]
        fx, bx = jnp.maximum(along, 0.0) * energy, jnp.minimum(along, 0.0) * energy
        across = group * sine + fields[2]
        fy, by = jnp.maximum(across, 0.0) * energy, jnp.minimum(across, 0.0) * energy
        turn = sine * fields[3] - cosine * fields[4]
        ft, bt = jnp.maximum(turn, 0.0) * energy, jnp.minimum(turn, 0.0) * energy
        edges[0, pl.ds(j, 1), :] = fx[ROWS - 1 :, :]
        edges[1, pl.ds(j, 1), :] = bx[:1, :]
        prev_x = jnp.where(rows == 0, 0.0, pltpu.roll(fx, 1, 0))
        next_x = jnp.where(rows == ROWS - 1, 0.0, pltpu.roll(bx, ROWS - 1, 0))
        prev_y = jnp.where(lanes == 0, 0.0, pltpu.roll(fy, 1, 1))
        next_y = jnp.where(lanes == COLS - 1, 0.0, pltpu.roll(by, COLS - 1, 1))
        change = (fx + next_x - (prev_x + bx)) + (fy + next_y - (prev_y + by)) + (ft - bt)
        wind = jnp.maximum(cosine * fields[5] + sine * fields[6], 0.0) * energy
        base[j] = energy - change + wind
        ahead[j + 1] = ft
        behind[j] = bt
        beside(j)
        return carry

    lax.fori_loop(lo, hi, one, 0)


def quad_masks(table_ref, mask_ref, z, j):
    def wrapped(turn):
        at = j + turn
        return jnp.where(at < 0, at + NDIR, jnp.where(at >= NDIR, at - NDIR, at))

    for row in range(4):
        turns = [wrapped(turn) for turn in ROW_DIRS[row]]
        for f in range(NY_DEV):
            freq = z * NY_DEV + f
            near = jnp.clip(freq + 2 * ROW_SIGN[row], 0, NFREQ - 1)
            far = jnp.clip(freq + 3 * ROW_SIGN[row], 0, NFREQ - 1)
            far = jnp.where(far == near, -NFREQ, far)
            bins = table_ref[row, z * PLANE_BINS + f * NDIR + j]
            for step, target in enumerate((near, far)):
                for which in range(2):
                    at = ((row * 2 + step) * 2 + which) * PLANE_BINS + f * NDIR
                    mask_ref[at + j] = jnp.where(bins == target * NDIR + turns[which], 1.0, 0.0).astype(F32)


def quadruplets(table_ref, coupling_ref, decay, x, square, q_one, q_two, n, z):
    def one(j, carry):
        for f in range(NY_DEV):
            k = z * PLANE_BINS + f * NDIR + j
            energy = x[k]
            a, b = x[table_ref[0, k]], x[table_ref[1, k]]
            c, d = x[table_ref[2, k]], x[table_ref[3, k]]
            scaled = coupling_ref[k] * energy
            first = scaled * (energy * (a + b) - 2.0 * a * b)
            second = scaled * (energy * (c + d) - 2.0 * c * d)
            q_one[f * NDIR + j] = first
            q_two[f * NDIR + j] = second
            n[(HALO + f) * NDIR + j] = -2.0 * (first + second) - (decay[f] * square) * energy
        return carry

    lax.fori_loop(0, NDIR, one, 0)


def scatter(mask_ref, q_one, q_two, n, targets):
    def one(j, carry):
        source = {}
        for turns in ROW_DIRS:
            for turn in turns:
                at = j - turn
                source[turn] = jnp.where(at < 0, at + NDIR, jnp.where(at >= NDIR, at - NDIR, at))
        for t in targets:
            total = n[t * NDIR + j] if HALO <= t < HALO + NY_DEV else None
            for row in range(4):
                q = q_one if row < 2 else q_two
                for step in range(2):
                    f = t - HALO - ROW_SIGN[row] * (2 + step)
                    if not 0 <= f < NY_DEV:
                        continue
                    for which in range(2):
                        at = ((row * 2 + step) * 2 + which) * PLANE_BINS + f * NDIR
                        s = source[ROW_DIRS[row][which]]
                        term = mask_ref[at + s] * q[f * NDIR + s]
                        total = term if total is None else total + term
            n[t * NDIR + j] = total
        return carry

    lax.fori_loop(0, NDIR, one, 0)


def step_kernel(
    const_ref, table_ref, coupling_ref,
    spectrum_ref, depth_ref, current_ref, slope_ref, forcing_ref, angle_ref, land_ref,
    out_ref,
    fields, base, ahead, behind, edges, edge_in, slot_row, slot_lane, lane_ref, row_ref, ends_ref,
    packed, x, n, q_one, q_two, up_in, down_in, source, sums, mask_ref,
    own_sem, send_y, recv_y, send_up, recv_up, send_down, recv_down, send_mean, recv_mean, send_edge, recv_edge,
    send_cup, recv_cup, send_cdown, recv_cdown, send_back, recv_back,
):
    space, spec = lax.axis_index("space"), lax.axis_index("spec")
    z, y = spec // NY_DEV, spec % NY_DEV
    has_up, has_down = z < PLANES - 1, z > 0
    not_first, not_last = space > 0, space < 7

    def to(plane, row):
        return {"spec": plane * NY_DEV + row}

    def remote(src, dst, send, recv, device):
        return pltpu.make_async_remote_copy(
            src_ref=src, dst_ref=dst, send_sem=send, recv_sem=recv, device_id=device, device_id_type=pl.DeviceIdType.MESH
        )

    def signal(device):
        pl.semaphore_signal(barrier, inc=1, device_id=device, device_id_type=pl.DeviceIdType.MESH)

    barrier = pltpu.get_barrier_semaphore()
    for d in range(1, NY_DEV):
        signal(to(z, (y + d) % NY_DEV))
    for d in range(1, PLANES):
        signal(to((z + d) % PLANES, y))

    @pl.when(not_first)
    def _():
        signal({"space": space - 1})

    @pl.when(not_last)
    def _():
        signal({"space": space + 1})

    def bins(freq, c):
        return pl.ds(freq * NDIR + c * PART, PART)

    def eight(row):
        return pl.ds(pl.multiple_of(row * 8, 8), 8)

    def at(f, c):
        return x.at[bins(z * NY_DEV + f, c)]

    def along_y(d, c):
        row = (y + d) % NY_DEV
        src = packed.at[pl.ds(c * PART, PART), eight(row), :]
        return remote(src, at(y, c), send_y.at[d, c], recv_y.at[y, c], to(z, row))

    def from_y(d, c):
        f = (y + d) % NY_DEV
        return remote(at(f, c), at(f, c), send_y.at[d, c], recv_y.at[f, c], to(z, f))

    def up(f, c, src=None):
        src = at(f, c) if src is None else src
        return remote(src, at(f, c), send_up.at[f - 1, c], recv_up.at[f - 1, c], to(z + 1, y))

    def down(f, c, src=None):
        src = at(f, c) if src is None else src
        return remote(src, at(f, c), send_down.at[f, c], recv_down.at[f, c], to(z - 1, y))

    def forward(f, c, src=None):
        @pl.when(has_up & (f >= 1))
        def _():
            up(f, c, src).start()

        @pl.when(has_down & (f < HALO))
        def _():
            down(f, c, src).start()

    def own(c):
        return pltpu.make_async_copy(packed.at[pl.ds(c * PART, PART), eight(y), :], at(y, c), own_sem.at[c])

    packing(land_ref, lane_ref, row_ref, ends_ref)
    for c in range(NCH):
        pack(spectrum_ref, lane_ref, row_ref, packed, c * PART, (c + 1) * PART)
        if c == 0:
            pl.semaphore_wait(barrier, 2 + PLANES + not_first.astype(jnp.int32) + not_last.astype(jnp.int32))
        forward(y, c, packed.at[pl.ds(c * PART, PART), eight(y), :])
        for d in (1, 3, 2):
            along_y(d, c).start()
        own(c).start()

    transport_fields(
        const_ref[2 * NDIR + spec], const_ref[2 * NDIR + NFREQ + spec],
        depth_ref, current_ref, slope_ref, forcing_ref, angle_ref, fields,
    )
    for c in range(NCH):
        for d in (1, 3, 2):
            from_y(d, c).wait_recv()
            forward((y + d) % NY_DEV, c)
        transport(const_ref, spectrum_ref, land_ref, fields, base, ahead, behind, edges, c * PART, (c + 1) * PART,
                  lambda j: quad_masks(table_ref, mask_ref, z, j))
        own(c).wait()

    def edge(side):
        return remote(edges.at[side], edge_in.at[side], send_edge.at[side], recv_edge.at[side],
                      {"space": space + 1 if side == 0 else space - 1})

    @pl.when(not_last)
    def _():
        edge(0).start()

    @pl.when(not_first)
    def _():
        edge(1).start()

    def add_up(k, total):
        return total + x[z * PLANE_BINS + k]

    sums[z] = lax.fori_loop(0, PLANE_BINS, add_up, jnp.zeros((8, COLS), F32), unroll=8)

    def mean(d):
        return remote(sums.at[z], sums.at[z], send_mean.at[d], recv_mean.at[z], to((z + d) % PLANES, y))

    for d in range(1, PLANES):
        mean(d).start()
    ahead[0] = ahead[NDIR]
    behind[NDIR] = behind[0]
    unpacking(land_ref, slot_row, slot_lane)
    for d in range(1, PLANES):
        other = (z + d) % PLANES
        remote(sums.at[other], sums.at[other], send_mean.at[d], recv_mean.at[other], to(other, y)).wait_recv()
    square = jnp.sum(sums[...], axis=0) * (1.0 / (NFREQ * NDIR))
    square = square * square

    @pl.when(has_down)
    def _():
        for c in range(NCH):
            for f in range(1, NY_DEV):
                remote(at(f - NY_DEV, c), at(f - NY_DEV, c), send_up.at[f - 1, c], recv_up.at[f - 1, c], to(z - 1, y)).wait_recv()

    @pl.when(has_up)
    def _():
        for c in range(NCH):
            for f in range(HALO):
                remote(at(NY_DEV + f, c), at(NY_DEV + f, c), send_down.at[f, c], recv_down.at[f, c], to(z + 1, y)).wait_recv()

    decay = [const_ref[2 * NDIR + 2 * NFREQ + z * NY_DEV + f] for f in range(NY_DEV)]
    quadruplets(table_ref, coupling_ref, decay, x, square, q_one, q_two, n, z)
    scatter(mask_ref, q_one, q_two, n, (0, 1, 2, 7, 8, 9))

    def whole(freq):
        return pl.ds(freq * NDIR, NDIR)

    def give_up(f):
        return remote(n.at[whole(HALO + NY_DEV + f)], up_in.at[f], send_cup.at[f], recv_cup.at[f], to(z + 1, y))

    def give_down(f):
        return remote(n.at[whole(f - 1)], down_in.at[f - 1], send_cdown.at[f - 1], recv_cdown.at[f - 1], to(z - 1, y))

    for d in (2, 1, 3, 0):
        f = (y + d) % NY_DEV

        @pl.when(has_up & (f < HALO))
        def _():
            give_up(f).start()

        @pl.when(has_down & (f >= 1))
        def _():
            give_down(f).start()

    scatter(mask_ref, q_one, q_two, n, (3, 4, 5, 6))

    @pl.when(z == 0)
    def _():
        def fold(j, carry):
            n[HALO * NDIR + j] += n[j] + n[NDIR + j] + n[2 * NDIR + j]
            return carry

        lax.fori_loop(0, NDIR, fold, 0)

    @pl.when(z == PLANES - 1)
    def _():
        def fold(j, carry):
            n[6 * NDIR + j] += n[7 * NDIR + j] + n[8 * NDIR + j] + n[9 * NDIR + j]
            return carry

        lax.fori_loop(0, NDIR, fold, 0)

    def back(d):
        f = (y + d) % NY_DEV
        return remote(n.at[whole(HALO + f)], source.at[:, eight(y), :], send_back.at[d], recv_back.at[y], to(z, f))

    for d in (2, 1, 3, 0):
        f = (y + d) % NY_DEV

        @pl.when(has_down & (f < HALO))
        def _():
            remote(n.at[whole(HALO + NY_DEV + f)], up_in.at[f], send_cup.at[f], recv_cup.at[f], to(z - 1, y)).wait_recv()

            def add(j, carry):
                n[(HALO + f) * NDIR + j] += up_in[f, j]
                return carry

            lax.fori_loop(0, NDIR, add, 0, unroll=4)

        @pl.when(has_up & (f >= 1))
        def _():
            remote(n.at[whole(f - 1)], down_in.at[f - 1], send_cdown.at[f - 1], recv_cdown.at[f - 1], to(z + 1, y)).wait_recv()

            def add(j, carry):
                n[(HALO + f) * NDIR + j] += down_in[f - 1, j]
                return carry

            lax.fori_loop(0, NDIR, add, 0, unroll=4)

        if d:
            back(d).start()
        else:
            def keep(j, carry):
                source[j, eight(y), :] = n[(HALO + f) * NDIR + j]
                return carry

            lax.fori_loop(0, NDIR, keep, 0, unroll=4)

    for side, there in ((0, not_first), (1, not_last)):
        @pl.when(there)
        def _():
            remote(edges.at[side], edge_in.at[side], send_edge.at[side], recv_edge.at[side],
                   {"space": space - 1 if side == 0 else space + 1}).wait_recv()

        @pl.when(jnp.logical_not(there))
        def _():
            edge_in[side] = jnp.zeros((NDIR, COLS), F32)

    for d in (2, 1, 3):
        f = (y + d) % NY_DEV
        remote(n.at[whole(HALO)], source.at[:, eight(f), :], send_back.at[d], recv_back.at[f], to(z, f)).wait_recv()

    def finish(j, carry):
        base[j, 0:1, :] += edge_in[0, pl.ds(j, 1), :]
        base[j, ROWS - 1 :, :] -= edge_in[1, pl.ds(j, 1), :]
        for v in range(8):
            rows = slice(8 * v, 8 * v + 8)
            added = unpack_block(lambda q: source[j, 8 * q : 8 * q + 8, :], slot_row[rows, :], slot_lane[rows, :], v)
            moved = base[j, rows, :] + ahead[j, rows, :] - behind[j + 1, rows, :]
            out_ref[j, rows, :] = jnp.where(land_ref[rows, :] > 0, moved + added, 0.0)
        return carry

    lax.fori_loop(0, NDIR, finish, 0)

    for c in range(NCH):
        for d in range(1, NY_DEV):
            along_y(d, c).wait_send()

    @pl.when(has_up)
    def _():
        for c in range(NCH):
            for f in range(1, NY_DEV):
                up(f, c).wait_send()
        for f in range(HALO):
            give_up(f).wait_send()

    @pl.when(has_down)
    def _():
        for c in range(NCH):
            for f in range(HALO):
                down(f, c).wait_send()
        for f in range(1, NY_DEV):
            give_down(f).wait_send()

    for d in range(1, PLANES):
        mean(d).wait_send()
    for d in range(1, NY_DEV):
        back(d).wait_send()

    @pl.when(not_last)
    def _():
        edge(0).wait_send()

    @pl.when(not_first)
    def _():
        edge(1).wait_send()


def constants():
    heading = np.float32(2.0 * np.pi / NDIR) * np.arange(NDIR, dtype=np.float32)
    growth = 1.1 ** np.arange(NFREQ)
    parts = [np.cos(heading), np.sin(heading), 2.0 * np.pi * 0.04 * growth, np.sqrt(growth), 0.3 * (growth / growth[-1]) ** 2]
    return np.concatenate(parts).astype(np.float32)


def on_device(spectrum, sea_depth, current, depth_slope, wind_forcing, wind_angle, land_sea, quad_table, coupling):
    spectrum = spectrum.reshape(NDIR, ROWS, COLS)
    dma = pltpu.SemaphoreType.DMA
    tile = pltpu.VMEM((ROWS, COLS), jnp.int32)
    longer = pltpu.VMEM((NDIR + 1, ROWS, COLS), F32)
    edges = pltpu.VMEM((2, NDIR, COLS), F32)
    own_bins = pltpu.VMEM((PLANE_BINS, 8, COLS), F32)
    all_bins = pltpu.VMEM(((NY_DEV + 2 * HALO) * NDIR, 8, COLS), F32)
    halo = pltpu.VMEM((HALO, NDIR, 8, COLS), F32)
    packed = pltpu.VMEM((NDIR, PACKED, COLS), F32)
    out = pl.pallas_call(
        step_kernel,
        out_shape=jax.ShapeDtypeStruct((NDIR, ROWS, COLS), F32),
        in_specs=[SMEM] * 3 + [VMEM] * 7,
        out_specs=VMEM,
        scratch_shapes=[
            pltpu.VMEM((7, ROWS, COLS), F32), pltpu.VMEM((NDIR, ROWS, COLS), F32), longer, longer, edges, edges,
            tile, tile, tile, pltpu.VMEM((PACKED, COLS), jnp.int32), tile,
            packed, pltpu.VMEM((NFREQ * NDIR, 8, COLS), F32), all_bins, own_bins, own_bins, halo, halo, packed,
            pltpu.VMEM((PLANES, 8, COLS), F32), pltpu.SMEM((16 * PLANE_BINS,), F32),
            dma((NCH,)), dma((NY_DEV, NCH)), dma((NY_DEV, NCH)),
            dma((HALO, NCH)), dma((HALO, NCH)), dma((HALO, NCH)), dma((HALO, NCH)),
            dma((PLANES,)), dma((PLANES,)), dma((2,)), dma((2,)),
            dma((HALO,)), dma((HALO,)), dma((HALO,)), dma((HALO,)), dma((NY_DEV,)), dma((NY_DEV,)),
        ],
        compiler_params=pltpu.CompilerParams(vmem_limit_bytes=40 << 20, collective_id=0, has_side_effects=True),
    )(jnp.asarray(constants()), quad_table, coupling, spectrum, sea_depth, current, depth_slope, wind_forcing, wind_angle, land_sea)
    return out.reshape(1, NDIR, ROWS, COLS)


def solution(mesh):
    return jax.shard_map(
        on_device,
        mesh=mesh,
        in_specs=(
            P("spec", None, "space", None),
            P("space", None),
            P(None, "space", None),
            P(None, "space", None),
            P("space", None),
            P("space", None),
            P("space", None),
            P(),
            P(),
        ),
        out_specs=P("spec", None, "space", None),
        check_vma=False,
    )
```

time: 96.1 us -> 56.9 us (0.59)
  the two profiles are of different devices: /device:TPU:107 before, /device:TPU:26 now
where the time goes in v1:
time: 56.9 us; the launch traced here: 56.3 us
  Pallas kernels  47.2 us (83%)
  local copies, waits for them, and re-layouts  9.09 us (16%)
    pallas_call x1, Pallas kernels, on_device(): pl.pallas_call(step_kernel, out_shape=jax.ShapeDtypeStruct((NDIR, ROWS, C...  47.2 us
    unnamed x21, local copies, waits for them, and re-layouts  9.09 us

profile of v1, /device:TPU:26, one launch (start us, length us, event | category | flops | bytes accessed | tf_op | source)
XLA Modules:
  0.0 56.3 jit_solution(15821662909367407996)
XLA Ops:
  0.0 0.0 copy-start
  0.0 1.3 %copy-done = f32[1,36,64,128]{3,2,1,0:T(8,128)S(1)} copy-done((f32[1,36,64,128]{3,2,1,0:T(8,128)S(1)}, f32[1,36,64,128]{3,2,1,0:T(8,128)}, u32[]{:S(2)}) %copy-start) | copy-done | bytes 1179672
  1.3 0.0 copy-start.1
  1.3 0.8 %copy-done.1 = f32[2,64,128]{2,1,0:T(8,128)S(1)} copy-done((f32[2,64,128]{2,1,0:T(8,128)S(1)}, f32[2,64,128]{2,1,0:T(8,128)}, u32[]{:S(2)}) %copy-start.1) | copy-done | bytes 65560
  2.1 0.0 copy-start.2
  2.1 0.8 %copy-done.2 = f32[2,64,128]{2,1,0:T(8,128)S(1)} copy-done((f32[2,64,128]{2,1,0:T(8,128)S(1)}, f32[2,64,128]{2,1,0:T(8,128)}, u32[]{:S(2)}) %copy-start.2) | copy-done | bytes 65560
  3.0 0.0 copy-start.3
  3.0 0.8 %copy-done.3 = f32[64,128]{1,0:T(8,128)S(1)} copy-done((f32[64,128]{1,0:T(8,128)S(1)}, f32[64,128]{1,0:T(8,128)}, u32[]{:S(2)}) %copy-start.3) | copy-done | bytes 32792
  3.7 0.0 copy-start.4
  3.7 0.8 %copy-done.4 = f32[64,128]{1,0:T(8,128)S(1)} copy-done((f32[64,128]{1,0:T(8,128)S(1)}, f32[64,128]{1,0:T(8,128)}, u32[]{:S(2)}) %copy-start.4) | copy-done | bytes 32792
  4.5 0.0 copy-start.5
  4.5 0.8 %copy-done.5 = f32[64,128]{1,0:T(8,128)S(1)} copy-done((f32[64,128]{1,0:T(8,128)S(1)}, f32[64,128]{1,0:T(8,128)}, u32[]{:S(2)}) %copy-start.5) | copy-done | bytes 32792
  5.2 0.0 copy-start.6
  5.2 0.8 %copy-done.6 = s32[64,128]{1,0:T(8,128)S(1)} copy-done((s32[64,128]{1,0:T(8,128)S(1)}, s32[64,128]{1,0:T(8,128)}, u32[]{:S(2)}) %copy-start.6) | copy-done | bytes 32792
  6.0 0.0 copy-start.7
  6.0 0.7 %copy-done.7 = s32[4,1152]{1,0:T(4,128)S(1)} copy-done((s32[4,1152]{1,0:T(4,128)S(1)}, s32[4,1152]{1,0:T(4,128)}, u32[]{:S(2)}) %copy-start.7) | copy-done | bytes 18456
  6.7 0.0 copy-start.8
  6.7 0.7 %copy-done.8 = f32[1152]{0:T(1024)S(1)} copy-done((f32[1152]{0:T(1024)S(1)}, f32[1152]{0:T(1024)}, u32[]{:S(2)}) %copy-start.8) | copy-done | bytes 4632
  7.4 0.0 copy-start.9
  7.4 0.7 %copy-done.9 = f32[168]{0:T(256)S(1)} copy-done((f32[168]{0:T(256)S(1)}, f32[168]{0:T(256)}, u32[]{:S(2)}) %copy-start.9) | copy-done | bytes 696
  8.1 47.2 %shard_map.100 = f32[36,64,128]{2,1,0:T(8,128)S(1)} custom-call(f32[168]{0:T(256)S(1)} %copy-done.9, s32[4,1152]{1,0:T(4,128)S(1)} %copy-done.7, f32[1152]{0:T(1024)S(1)} %copy-done.8, f32[36,64,128]{2,1,0:T(8,128)S(1)} %bitcast.3, f32[64,128]{1,0:T(8,128)S(1)} %copy-done.3, f32[2,64,128]{2,1,0:T(8,128)S(1)} %copy-done.1, f32[2,64,128]{2,1,0:T(8,128)S(1)} %copy-done.2, ...), custom_call_target="tpu_custom_call" | custom-call | tf_op jit(solution)/shard_map/pallas_call | solution.py:495
  55.3 1.0 %copy.12 = f32[1,36,64,128]{3,2,1,0:T(8,128)} copy(f32[1,36,64,128]{3,2,1,0:T(8,128)S(1)} %bitcast.2) | data formatting | bytes 2359296
Async XLA Ops:
  0.0 1.3 %copy-start = (f32[1,36,64,128]{3,2,1,0:T(8,128)S(1)}, f32[1,36,64,128]{3,2,1,0:T(8,128)}, u32[]{:S(2)}) copy-start(f32[1,36,64,128]{3,2,1,0:T(8,128)} %param.10) | copy-start | bytes 3538948
  1.3 0.8 %copy-start.1 = (f32[2,64,128]{2,1,0:T(8,128)S(1)}, f32[2,64,128]{2,1,0:T(8,128)}, u32[]{:S(2)}) copy-start(f32[2,64,128]{2,1,0:T(8,128)} %current_ref.1) | copy-start | bytes 196612
  2.1 0.8 %copy-start.2 = (f32[2,64,128]{2,1,0:T(8,128)S(1)}, f32[2,64,128]{2,1,0:T(8,128)}, u32[]{:S(2)}) copy-start(f32[2,64,128]{2,1,0:T(8,128)} %slope_ref.1) | copy-start | bytes 196612
  3.0 0.8 %copy-start.3 = (f32[64,128]{1,0:T(8,128)S(1)}, f32[64,128]{1,0:T(8,128)}, u32[]{:S(2)}) copy-start(f32[64,128]{1,0:T(8,128)} %depth_ref.1) | copy-start | bytes 98308
  3.7 0.8 %copy-start.4 = (f32[64,128]{1,0:T(8,128)S(1)}, f32[64,128]{1,0:T(8,128)}, u32[]{:S(2)}) copy-start(f32[64,128]{1,0:T(8,128)} %forcing_ref.1) | copy-start | bytes 98308
  4.5 0.8 %copy-start.5 = (f32[64,128]{1,0:T(8,128)S(1)}, f32[64,128]{1,0:T(8,128)}, u32[]{:S(2)}) copy-start(f32[64,128]{1,0:T(8,128)} %angle_ref.1) | copy-start | bytes 98308
  5.2 0.8 %copy-start.6 = (s32[64,128]{1,0:T(8,128)S(1)}, s32[64,128]{1,0:T(8,128)}, u32[]{:S(2)}) copy-start(s32[64,128]{1,0:T(8,128)} %land_ref.1) | copy-start | bytes 98308
  6.0 0.7 %copy-start.7 = (s32[4,1152]{1,0:T(4,128)S(1)}, s32[4,1152]{1,0:T(4,128)}, u32[]{:S(2)}) copy-start(s32[4,1152]{1,0:T(4,128)} %table_ref.1) | copy-start | bytes 55300
  6.7 0.7 %copy-start.8 = (f32[1152]{0:T(1024)S(1)}, f32[1152]{0:T(1024)}, u32[]{:S(2)}) copy-start(f32[1152]{0:T(1024)} %coupling_ref.1) | copy-start | bytes 13828
  7.4 0.7 %copy-start.9 = (f32[168]{0:T(256)S(1)}, f32[168]{0:T(256)}, u32[]{:S(2)}) copy-start(f32[168]{0:T(256)} %constant.2.clone.const_ref) | copy-start | bytes 2020

commit v2 on v1

--- a/solution.py
+++ b/solution.py
@@ -151,7 +151,7 @@
                     mask_ref[at + j] = jnp.where(bins == target * NDIR + turns[which], 1.0, 0.0).astype(F32)
 
 
-def quadruplets(table_ref, coupling_ref, decay, x, square, q_one, q_two, n, z):
+def quadruplets(table_ref, coupling_ref, x, q_one, q_two, n, z):
     def one(j, carry):
         for f in range(NY_DEV):
             k = z * PLANE_BINS + f * NDIR + j
@@ -163,13 +163,22 @@
             second = scaled * (energy * (c + d) - 2.0 * c * d)
             q_one[f * NDIR + j] = first
             q_two[f * NDIR + j] = second
-            n[(HALO + f) * NDIR + j] = -2.0 * (first + second) - (decay[f] * square) * energy
+            n[(HALO + f) * NDIR + j] = -2.0 * (first + second)
         return carry
 
     lax.fori_loop(0, NDIR, one, 0)
 
 
-def scatter(mask_ref, q_one, q_two, n, targets):
+def decline(decay, square, x, n, z):
+    def one(j, carry):
+        for f in range(NY_DEV):
+            n[(HALO + f) * NDIR + j] -= (decay[f] * square) * x[z * PLANE_BINS + f * NDIR + j]
+        return carry
+
+    lax.fori_loop(0, NDIR, one, 0)
+
+
+def scatter(mask_ref, q_one, q_two, n, targets, lo, hi):
     def one(j, carry):
         source = {}
         for turns in ROW_DIRS:
@@ -192,15 +201,18 @@
             n[t * NDIR + j] = total
         return carry
 
-    lax.fori_loop(0, NDIR, one, 0)
+    lax.fori_loop(lo, hi, one, 0)
 
 
 def step_kernel(
+    const_hbm, table_hbm, coupling_hbm,
+    spectrum_hbm, depth_hbm, current_hbm, slope_hbm, forcing_hbm, angle_hbm, land_hbm,
+    out_ref,
     const_ref, table_ref, coupling_ref,
     spectrum_ref, depth_ref, current_ref, slope_ref, forcing_ref, angle_ref, land_ref,
-    out_ref,
     fields, base, ahead, behind, edges, edge_in, slot_row, slot_lane, lane_ref, row_ref, ends_ref,
-    packed, x, n, q_one, q_two, up_in, down_in, source, sums, mask_ref,
+    packed, x, n, q_one, q_two, up_in, down_in, source, sums, sums_in, mask_ref,
+    load_sem, part_sem,
     own_sem, send_y, recv_y, send_up, recv_up, send_down, recv_down, send_mean, recv_mean, send_edge, recv_edge,
     send_cup, recv_cup, send_cdown, recv_cdown, send_back, recv_back,
 ):
@@ -220,19 +232,47 @@
     def signal(device):
         pl.semaphore_signal(barrier, inc=1, device_id=device, device_id_type=pl.DeviceIdType.MESH)
 
+    def spectrum_load(c):
+        part = pl.ds(c * PART, PART)
+        return pltpu.make_async_copy(spectrum_hbm.at[part], spectrum_ref.at[part], part_sem.at[c])
+
+    pairs = (
+        (land_hbm, land_ref), (const_hbm, const_ref), (depth_hbm, depth_ref), (current_hbm, current_ref),
+        (slope_hbm, slope_ref), (forcing_hbm, forcing_ref), (angle_hbm, angle_ref), (table_hbm, table_ref),
+        (coupling_hbm, coupling_ref),
+    )
+    loads = [pltpu.make_async_copy(src, dst, load_sem.at[i]) for i, (src, dst) in enumerate(pairs)]
+    loads[0].start()
+    for c in range(NCH):
+        spectrum_load(c).start()
+    for load in loads[1:]:
+        load.start()
+
     barrier = pltpu.get_barrier_semaphore()
+    even = space % 2 == 0
+    in_spec = NY_DEV - 1 + has_up.astype(jnp.int32) + has_down.astype(jnp.int32)
+    in_space = not_first.astype(jnp.int32) + not_last.astype(jnp.int32)
     for d in range(1, NY_DEV):
         signal(to(z, (y + d) % NY_DEV))
-    for d in range(1, PLANES):
-        signal(to((z + d) % PLANES, y))
-
-    @pl.when(not_first)
-    def _():
-        signal({"space": space - 1})
-
-    @pl.when(not_last)
-    def _():
-        signal({"space": space + 1})
+
+    @pl.when(has_up)
+    def _():
+        signal(to(z + 1, y))
+
+    @pl.when(has_down)
+    def _():
+        signal(to(z - 1, y))
+
+    def greet():
+        pl.semaphore_wait(barrier, in_spec + jnp.where(even, 0, in_space))
+
+        @pl.when(not_first)
+        def _():
+            signal({"space": space - 1})
+
+        @pl.when(not_last)
+        def _():
+            signal({"space": space + 1})
 
     def bins(freq, c):
         return pl.ds(freq * NDIR + c * PART, PART)
@@ -272,16 +312,20 @@
     def own(c):
         return pltpu.make_async_copy(packed.at[pl.ds(c * PART, PART), eight(y), :], at(y, c), own_sem.at[c])
 
+    loads[0].wait()
     packing(land_ref, lane_ref, row_ref, ends_ref)
     for c in range(NCH):
+        spectrum_load(c).wait()
         pack(spectrum_ref, lane_ref, row_ref, packed, c * PART, (c + 1) * PART)
         if c == 0:
-            pl.semaphore_wait(barrier, 2 + PLANES + not_first.astype(jnp.int32) + not_last.astype(jnp.int32))
+            greet()
         forward(y, c, packed.at[pl.ds(c * PART, PART), eight(y), :])
         for d in (1, 3, 2):
             along_y(d, c).start()
         own(c).start()
 
+    for load in loads[1:]:
+        load.wait()
     transport_fields(
         const_ref[2 * NDIR + spec], const_ref[2 * NDIR + NFREQ + spec],
         depth_ref, current_ref, slope_ref, forcing_ref, angle_ref, fields,
@@ -298,6 +342,10 @@
         return remote(edges.at[side], edge_in.at[side], send_edge.at[side], recv_edge.at[side],
                       {"space": space + 1 if side == 0 else space - 1})
 
+    @pl.when(even)
+    def _():
+        pl.semaphore_wait(barrier, in_space)
+
     @pl.when(not_last)
     def _():
         edge(0).start()
@@ -309,21 +357,47 @@
     def add_up(k, total):
         return total + x[z * PLANE_BINS + k]
 
-    sums[z] = lax.fori_loop(0, PLANE_BINS, add_up, jnp.zeros((8, COLS), F32), unroll=8)
-
-    def mean(d):
-        return remote(sums.at[z], sums.at[z], send_mean.at[d], recv_mean.at[z], to((z + d) % PLANES, y))
-
-    for d in range(1, PLANES):
-        mean(d).start()
+    total = lax.fori_loop(0, PLANE_BINS, add_up, jnp.zeros((8, COLS), F32), unroll=8)
+    sums[0, 0] = total
+    sums[1, 0] = total
+
+    def across(stage, way):
+        step = 1 << stage
+        other = z + step if way == 0 else z - step
+        there = (other < PLANES) if way == 0 else (other >= 0)
+        comes = (z >= step) if way == 0 else (z + step < PLANES)
+        copy = remote(
+            sums.at[way, stage], sums_in.at[way, stage], send_mean.at[way, stage], recv_mean.at[way, stage], to(other, y)
+        )
+        return there, comes, copy
+
+    def sums_out(stage):
+        for way in range(2):
+            there, _, copy = across(stage, way)
+
+            @pl.when(there)
+            def _():
+                copy.start()
+
+    def sums_come(stage):
+        for way in range(2):
+            _, comes, copy = across(stage, way)
+
+            @pl.when(comes)
+            def _():
+                copy.wait_recv()
+                sums[way, stage + 1] = sums[way, stage] + sums_in[way, stage]
+
+            @pl.when(jnp.logical_not(comes))
+            def _():
+                sums[way, stage + 1] = sums[way, stage]
+
+    sums_out(0)
     ahead[0] = ahead[NDIR]
     behind[NDIR] = behind[0]
     unpacking(land_ref, slot_row, slot_lane)
-    for d in range(1, PLANES):
-        other = (z + d) % PLANES
-        remote(sums.at[other], sums.at[other], send_mean.at[d], recv_mean.at[other], to(other, y)).wait_recv()
-    square = jnp.sum(sums[...], axis=0) * (1.0 / (NFREQ * NDIR))
-    square = square * square
+    sums_come(0)
+    sums_out(1)
 
     @pl.when(has_down)
     def _():
@@ -337,31 +411,30 @@
             for f in range(HALO):
                 remote(at(NY_DEV + f, c), at(NY_DEV + f, c), send_down.at[f, c], recv_down.at[f, c], to(z + 1, y)).wait_recv()
 
-    decay = [const_ref[2 * NDIR + 2 * NFREQ + z * NY_DEV + f] for f in range(NY_DEV)]
-    quadruplets(table_ref, coupling_ref, decay, x, square, q_one, q_two, n, z)
-    scatter(mask_ref, q_one, q_two, n, (0, 1, 2, 7, 8, 9))
-
-    def whole(freq):
-        return pl.ds(freq * NDIR, NDIR)
-
-    def give_up(f):
-        return remote(n.at[whole(HALO + NY_DEV + f)], up_in.at[f], send_cup.at[f], recv_cup.at[f], to(z + 1, y))
-
-    def give_down(f):
-        return remote(n.at[whole(f - 1)], down_in.at[f - 1], send_cdown.at[f - 1], recv_cdown.at[f - 1], to(z - 1, y))
-
-    for d in (2, 1, 3, 0):
-        f = (y + d) % NY_DEV
-
-        @pl.when(has_up & (f < HALO))
-        def _():
-            give_up(f).start()
-
-        @pl.when(has_down & (f >= 1))
-        def _():
-            give_down(f).start()
-
-    scatter(mask_ref, q_one, q_two, n, (3, 4, 5, 6))
+    sums_come(1)
+    sums_out(2)
+    quadruplets(table_ref, coupling_ref, x, q_one, q_two, n, z)
+
+    def give_up(f, c):
+        return remote(n.at[bins(HALO + NY_DEV + f, c)], up_in.at[bins(f, c)], send_cup.at[f, c], recv_cup.at[f, c], to(z + 1, y))
+
+    def give_down(f, c):
+        return remote(n.at[bins(f - 1, c)], down_in.at[bins(f - 1, c)], send_cdown.at[f - 1, c], recv_cdown.at[f - 1, c], to(z - 1, y))
+
+    for c in range(NCH):
+        scatter(mask_ref, q_one, q_two, n, (0, 1, 2, 7, 8, 9), c * PART, (c + 1) * PART)
+
+        @pl.when(has_up)
+        def _():
+            for f in range(HALO):
+                give_up(f, c).start()
+
+        @pl.when(has_down)
+        def _():
+            for f in range(1, NY_DEV):
+                give_down(f, c).start()
+
+    scatter(mask_ref, q_one, q_two, n, (3, 4, 5, 6), 0, NDIR)
 
     @pl.when(z == 0)
     def _():
@@ -379,41 +452,10 @@
 
         lax.fori_loop(0, NDIR, fold, 0)
 
-    def back(d):
-        f = (y + d) % NY_DEV
-        return remote(n.at[whole(HALO + f)], source.at[:, eight(y), :], send_back.at[d], recv_back.at[y], to(z, f))
-
-    for d in (2, 1, 3, 0):
-        f = (y + d) % NY_DEV
-
-        @pl.when(has_down & (f < HALO))
-        def _():
-            remote(n.at[whole(HALO + NY_DEV + f)], up_in.at[f], send_cup.at[f], recv_cup.at[f], to(z - 1, y)).wait_recv()
-
-            def add(j, carry):
-                n[(HALO + f) * NDIR + j] += up_in[f, j]
-                return carry
-
-            lax.fori_loop(0, NDIR, add, 0, unroll=4)
-
-        @pl.when(has_up & (f >= 1))
-        def _():
-            remote(n.at[whole(f - 1)], down_in.at[f - 1], send_cdown.at[f - 1], recv_cdown.at[f - 1], to(z + 1, y)).wait_recv()
-
-            def add(j, carry):
-                n[(HALO + f) * NDIR + j] += down_in[f - 1, j]
-                return carry
-
-            lax.fori_loop(0, NDIR, add, 0, unroll=4)
-
-        if d:
-            back(d).start()
-        else:
-            def keep(j, carry):
-                source[j, eight(y), :] = n[(HALO + f) * NDIR + j]
-                return carry
-
-            lax.fori_loop(0, NDIR, keep, 0, unroll=4)
+    sums_come(2)
+    square = (sums[0, 3] + sums[1, 3] - sums[0, 0]) * (1.0 / (NFREQ * NDIR))
+    square = square * square
+    decline([const_ref[2 * NDIR + 2 * NFREQ + z * NY_DEV + f] for f in range(NY_DEV)], square, x, n, z)
 
     for side, there in ((0, not_first), (1, not_last)):
         @pl.when(there)
@@ -425,9 +467,9 @@
         def _():
             edge_in[side] = jnp.zeros((NDIR, COLS), F32)
 
-    for d in (2, 1, 3):
+    def back(d, c):
         f = (y + d) % NY_DEV
-        remote(n.at[whole(HALO)], source.at[:, eight(f), :], send_back.at[d], recv_back.at[f], to(z, f)).wait_recv()
+        return remote(n.at[bins(HALO + f, c)], source.at[pl.ds(c * PART, PART), eight(y), :], send_back.at[d, c], recv_back.at[y, c], to(z, f))
 
     def finish(j, carry):
         base[j, 0:1, :] += edge_in[0, pl.ds(j, 1), :]
@@ -439,7 +481,54 @@
             out_ref[j, rows, :] = jnp.where(land_ref[rows, :] > 0, moved + added, 0.0)
         return carry
 
-    lax.fori_loop(0, NDIR, finish, 0)
+    def complete(c):
+        @pl.when(has_down)
+        def _():
+            for f in range(HALO):
+                at_n = n.at[bins(HALO + NY_DEV + f, c)]
+                remote(at_n, up_in.at[bins(f, c)], send_cup.at[f, c], recv_cup.at[f, c], to(z - 1, y)).wait_recv()
+
+            def add(j, carry):
+                for f in range(HALO):
+                    n[(HALO + f) * NDIR + j] += up_in[f * NDIR + j]
+                return carry
+
+            lax.fori_loop(c * PART, (c + 1) * PART, add, 0)
+
+        @pl.when(has_up)
+        def _():
+            for f in range(1, NY_DEV):
+                at_n = n.at[bins(f - 1, c)]
+                remote(at_n, down_in.at[bins(f - 1, c)], send_cdown.at[f - 1, c], recv_cdown.at[f - 1, c], to(z + 1, y)).wait_recv()
+
+            def add(j, carry):
+                for f in range(1, NY_DEV):
+                    n[(HALO + f) * NDIR + j] += down_in[(f - 1) * NDIR + j]
+                return carry
+
+            lax.fori_loop(c * PART, (c + 1) * PART, add, 0)
+
+        for d in (2, 1, 3):
+            back(d, c).start()
+
+        def keep(j, carry):
+            source[j, eight(y), :] = n[(HALO + y) * NDIR + j]
+            return carry
+
+        lax.fori_loop(c * PART, (c + 1) * PART, keep, 0)
+
+    def conclude(c):
+        for d in (1, 3, 2):
+            f = (y + d) % NY_DEV
+            at_source = source.at[pl.ds(c * PART, PART), eight(f), :]
+            remote(n.at[bins(HALO, c)], at_source, send_back.at[d, c], recv_back.at[f, c], to(z, f)).wait_recv()
+        lax.fori_loop(c * PART, (c + 1) * PART, finish, 0)
+
+    for c in range(NCH):
+        complete(c)
+        if c:
+            conclude(c - 1)
+    conclude(NCH - 1)
 
     for c in range(NCH):
         for d in range(1, NY_DEV):
@@ -450,21 +539,28 @@
         for c in range(NCH):
             for f in range(1, NY_DEV):
                 up(f, c).wait_send()
-        for f in range(HALO):
-            give_up(f).wait_send()
+            for f in range(HALO):
+                give_up(f, c).wait_send()
 
     @pl.when(has_down)
     def _():
         for c in range(NCH):
             for f in range(HALO):
                 down(f, c).wait_send()
-        for f in range(1, NY_DEV):
-            give_down(f).wait_send()
-
-    for d in range(1, PLANES):
-        mean(d).wait_send()
-    for d in range(1, NY_DEV):
-        back(d).wait_send()
+            for f in range(1, NY_DEV):
+                give_down(f, c).wait_send()
+
+    for stage in range(3):
+        for way in range(2):
+            there, _, copy = across(stage, way)
+
+            @pl.when(there)
+            def _():
+                copy.wait_send()
+
+    for c in range(NCH):
+        for d in range(1, NY_DEV):
+            back(d, c).wait_send()
 
     @pl.when(not_last)
     def _():
@@ -485,27 +581,30 @@
 def on_device(spectrum, sea_depth, current, depth_slope, wind_forcing, wind_angle, land_sea, quad_table, coupling):
     spectrum = spectrum.reshape(NDIR, ROWS, COLS)
     dma = pltpu.SemaphoreType.DMA
-    tile = pltpu.VMEM((ROWS, COLS), jnp.int32)
+    tile, field, two = pltpu.VMEM((ROWS, COLS), jnp.int32), pltpu.VMEM((ROWS, COLS), F32), pltpu.VMEM((2, ROWS, COLS), F32)
     longer = pltpu.VMEM((NDIR + 1, ROWS, COLS), F32)
     edges = pltpu.VMEM((2, NDIR, COLS), F32)
     own_bins = pltpu.VMEM((PLANE_BINS, 8, COLS), F32)
     all_bins = pltpu.VMEM(((NY_DEV + 2 * HALO) * NDIR, 8, COLS), F32)
-    halo = pltpu.VMEM((HALO, NDIR, 8, COLS), F32)
+    halo = pltpu.VMEM((HALO * NDIR, 8, COLS), F32)
     packed = pltpu.VMEM((NDIR, PACKED, COLS), F32)
     out = pl.pallas_call(
         step_kernel,
         out_shape=jax.ShapeDtypeStruct((NDIR, ROWS, COLS), F32),
-        in_specs=[SMEM] * 3 + [VMEM] * 7,
+        in_specs=[pl.BlockSpec(memory_space=pltpu.HBM)] * 10,
         out_specs=VMEM,
         scratch_shapes=[
+            pltpu.SMEM((2 * NDIR + 3 * NFREQ,), F32), pltpu.SMEM((4, NFREQ * NDIR), jnp.int32), pltpu.SMEM((NFREQ * NDIR,), F32),
+            pltpu.VMEM((NDIR, ROWS, COLS), F32), field, two, two, field, field, tile,
             pltpu.VMEM((7, ROWS, COLS), F32), pltpu.VMEM((NDIR, ROWS, COLS), F32), longer, longer, edges, edges,
             tile, tile, tile, pltpu.VMEM((PACKED, COLS), jnp.int32), tile,
             packed, pltpu.VMEM((NFREQ * NDIR, 8, COLS), F32), all_bins, own_bins, own_bins, halo, halo, packed,
-            pltpu.VMEM((PLANES, 8, COLS), F32), pltpu.SMEM((16 * PLANE_BINS,), F32),
+            pltpu.VMEM((2, 4, 8, COLS), F32), pltpu.VMEM((2, 3, 8, COLS), F32), pltpu.SMEM((16 * PLANE_BINS,), F32),
+            dma((9,)), dma((NCH,)),
             dma((NCH,)), dma((NY_DEV, NCH)), dma((NY_DEV, NCH)),
             dma((HALO, NCH)), dma((HALO, NCH)), dma((HALO, NCH)), dma((HALO, NCH)),
-            dma((PLANES,)), dma((PLANES,)), dma((2,)), dma((2,)),
-            dma((HALO,)), dma((HALO,)), dma((HALO,)), dma((HALO,)), dma((NY_DEV,)), dma((NY_DEV,)),
+            dma((2, 3)), dma((2, 3)), dma((2,)), dma((2,)),
+            dma((HALO, NCH)), dma((HALO, NCH)), dma((HALO, NCH)), dma((HALO, NCH)), dma((NY_DEV, NCH)), dma((NY_DEV, NCH)),
         ],
         compiler_params=pltpu.CompilerParams(vmem_limit_bytes=40 << 20, collective_id=0, has_side_effects=True),
     )(jnp.asarray(constants()), quad_table, coupling, spectrum, sea_depth, current, depth_slope, wind_forcing, wind_angle, land_sea)

time: 56.9 us -> 59.1 us (1.039)
  the two profiles are of different devices: /device:TPU:26 before, /device:TPU:6 now
where the time goes in v2:
time: 59.1 us; the launch traced here: 58.5 us
  Pallas kernels  49.4 us (84%)
  local copies, waits for them, and re-layouts  9.09 us (15%)
    pallas_call x1, Pallas kernels, on_device(): pl.pallas_call(step_kernel, out_shape=jax.ShapeDtypeStruct((NDIR, ROWS, C...  49.4 us
    unnamed x21, local copies, waits for them, and re-layouts  9.09 us

profile of v2, /device:TPU:6, one launch (start us, length us, event | category | flops | bytes accessed | tf_op | source)
XLA Modules:
  0.0 58.5 jit_solution(1330284956989506053)
XLA Ops:
  0.0 0.0 copy-start
  0.0 1.3 %copy-done = f32[1,36,64,128]{3,2,1,0:T(8,128)S(1)} copy-done((f32[1,36,64,128]{3,2,1,0:T(8,128)S(1)}, f32[1,36,64,128]{3,2,1,0:T(8,128)}, u32[]{:S(2)}) %copy-start) | copy-done | bytes 1179672
  1.3 0.0 copy-start.1
  1.3 0.8 %copy-done.1 = f32[2,64,128]{2,1,0:T(8,128)S(1)} copy-done((f32[2,64,128]{2,1,0:T(8,128)S(1)}, f32[2,64,128]{2,1,0:T(8,128)}, u32[]{:S(2)}) %copy-start.1) | copy-done | bytes 65560
  2.1 0.0 copy-start.2
  2.1 0.8 %copy-done.2 = f32[2,64,128]{2,1,0:T(8,128)S(1)} copy-done((f32[2,64,128]{2,1,0:T(8,128)S(1)}, f32[2,64,128]{2,1,0:T(8,128)}, u32[]{:S(2)}) %copy-start.2) | copy-done | bytes 65560
  3.0 0.0 copy-start.3
  3.0 0.8 %copy-done.3 = f32[64,128]{1,0:T(8,128)S(1)} copy-done((f32[64,128]{1,0:T(8,128)S(1)}, f32[64,128]{1,0:T(8,128)}, u32[]{:S(2)}) %copy-start.3) | copy-done | bytes 32792
  3.7 0.0 copy-start.4
  3.7 0.8 %copy-done.4 = f32[64,128]{1,0:T(8,128)S(1)} copy-done((f32[64,128]{1,0:T(8,128)S(1)}, f32[64,128]{1,0:T(8,128)}, u32[]{:S(2)}) %copy-start.4) | copy-done | bytes 32792
  4.5 0.0 copy-start.5
  4.5 0.8 %copy-done.5 = f32[64,128]{1,0:T(8,128)S(1)} copy-done((f32[64,128]{1,0:T(8,128)S(1)}, f32[64,128]{1,0:T(8,128)}, u32[]{:S(2)}) %copy-start.5) | copy-done | bytes 32792
  5.2 0.0 copy-start.6
  5.2 0.8 %copy-done.6 = s32[64,128]{1,0:T(8,128)S(1)} copy-done((s32[64,128]{1,0:T(8,128)S(1)}, s32[64,128]{1,0:T(8,128)}, u32[]{:S(2)}) %copy-start.6) | copy-done | bytes 32792
  6.0 0.0 copy-start.7
  6.0 0.7 %copy-done.7 = s32[4,1152]{1,0:T(4,128)S(1)} copy-done((s32[4,1152]{1,0:T(4,128)S(1)}, s32[4,1152]{1,0:T(4,128)}, u32[]{:S(2)}) %copy-start.7) | copy-done | bytes 18456
  6.7 0.0 copy-start.8
  6.7 0.7 %copy-done.8 = f32[1152]{0:T(1024)S(1)} copy-done((f32[1152]{0:T(1024)S(1)}, f32[1152]{0:T(1024)}, u32[]{:S(2)}) %copy-start.8) | copy-done | bytes 4632
  7.4 0.0 copy-start.9
  7.4 0.7 %copy-done.9 = f32[168]{0:T(256)S(1)} copy-done((f32[168]{0:T(256)S(1)}, f32[168]{0:T(256)}, u32[]{:S(2)}) %copy-start.9) | copy-done | bytes 696
  8.1 49.4 %shard_map.100 = f32[36,64,128]{2,1,0:T(8,128)S(1)} custom-call(f32[168]{0:T(256)S(1)} %copy-done.9, s32[4,1152]{1,0:T(4,128)S(1)} %copy-done.7, f32[1152]{0:T(1024)S(1)} %copy-done.8, f32[36,64,128]{2,1,0:T(8,128)S(1)} %bitcast.3, f32[64,128]{1,0:T(8,128)S(1)} %copy-done.3, f32[2,64,128]{2,1,0:T(8,128)S(1)} %copy-done.1, f32[2,64,128]{2,1,0:T(8,128)S(1)} %copy-done.2, ...), custom_call_target="tpu_custom_call" | custom-call | tf_op jit(solution)/shard_map/pallas_call | solution.py:591
  57.5 1.0 %copy.12 = f32[1,36,64,128]{3,2,1,0:T(8,128)} copy(f32[1,36,64,128]{3,2,1,0:T(8,128)S(1)} %bitcast.2) | data formatting | bytes 2359296
Async XLA Ops:
  0.0 1.3 %copy-start = (f32[1,36,64,128]{3,2,1,0:T(8,128)S(1)}, f32[1,36,64,128]{3,2,1,0:T(8,128)}, u32[]{:S(2)}) copy-start(f32[1,36,64,128]{3,2,1,0:T(8,128)} %param.10) | copy-start | bytes 3538948
  1.3 0.8 %copy-start.1 = (f32[2,64,128]{2,1,0:T(8,128)S(1)}, f32[2,64,128]{2,1,0:T(8,128)}, u32[]{:S(2)}) copy-start(f32[2,64,128]{2,1,0:T(8,128)} %current_hbm.1) | copy-start | bytes 196612
  2.1 0.8 %copy-start.2 = (f32[2,64,128]{2,1,0:T(8,128)S(1)}, f32[2,64,128]{2,1,0:T(8,128)}, u32[]{:S(2)}) copy-start(f32[2,64,128]{2,1,0:T(8,128)} %slope_hbm.1) | copy-start | bytes 196612
  3.0 0.8 %copy-start.3 = (f32[64,128]{1,0:T(8,128)S(1)}, f32[64,128]{1,0:T(8,128)}, u32[]{:S(2)}) copy-start(f32[64,128]{1,0:T(8,128)} %depth_hbm.1) | copy-start | bytes 98308
  3.7 0.8 %copy-start.4 = (f32[64,128]{1,0:T(8,128)S(1)}, f32[64,128]{1,0:T(8,128)}, u32[]{:S(2)}) copy-start(f32[64,128]{1,0:T(8,128)} %forcing_hbm.1) | copy-start | bytes 98308
  4.5 0.8 %copy-start.5 = (f32[64,128]{1,0:T(8,128)S(1)}, f32[64,128]{1,0:T(8,128)}, u32[]{:S(2)}) copy-start(f32[64,128]{1,0:T(8,128)} %angle_hbm.1) | copy-start | bytes 98308
  5.2 0.8 %copy-start.6 = (s32[64,128]{1,0:T(8,128)S(1)}, s32[64,128]{1,0:T(8,128)}, u32[]{:S(2)}) copy-start(s32[64,128]{1,0:T(8,128)} %land_hbm.1) | copy-start | bytes 98308
  6.0 0.7 %copy-start.7 = (s32[4,1152]{1,0:T(4,128)S(1)}, s32[4,1152]{1,0:T(4,128)}, u32[]{:S(2)}) copy-start(s32[4,1152]{1,0:T(4,128)} %table_hbm.1) | copy-start | bytes 55300
  6.7 0.7 %copy-start.8 = (f32[1152]{0:T(1024)S(1)}, f32[1152]{0:T(1024)}, u32[]{:S(2)}) copy-start(f32[1152]{0:T(1024)} %coupling_hbm.1) | copy-start | bytes 13828
  7.4 0.7 %copy-start.9 = (f32[168]{0:T(256)S(1)}, f32[168]{0:T(256)}, u32[]{:S(2)}) copy-start(f32[168]{0:T(256)} %constant.2.clone.const_hbm) | copy-start | bytes 2020

commit v3 on v2

--- a/solution.py
+++ b/solution.py
@@ -11,8 +11,8 @@
 PACKED = 32
 PLANES = NFREQ // NY_DEV
 HALO = 3
-NCH = 3
-PART = NDIR // NCH
+IN_PARTS = ((0, 6), (6, 12), (18, 18))
+OUT_PARTS = ((0, 16), (16, 14), (30, 6))
 PLANE_BINS = NY_DEV * NDIR
 F32 = jnp.float32
 VMEM = pl.BlockSpec(memory_space=pltpu.VMEM)
@@ -55,9 +55,9 @@
     row_ref[...] = lax.fori_loop(0, ROWS, count_row, jnp.zeros((PACKED, COLS), jnp.int32), unroll=8)
 
 
-def pack(spectrum_ref, lane_ref, row_ref, packed_ref, lo, hi):
+def pack(spectrum_ref, lane_ref, row_ref, packed_ref, lo, hi, sums):
     def one(d, carry):
-        staged = []
+        carry, staged = list(carry), []
         for v in range(8):
             rows = slice(8 * v, 8 * v + 8)
             staged.append(jnp.take_along_axis(spectrum_ref[d, rows, :], lane_ref[rows, :], axis=1))
@@ -69,9 +69,10 @@
             for v in range(q, 8):
                 out = jnp.where(block == v, jnp.take_along_axis(staged[v], within, axis=0), out)
             packed_ref[d, rows, :] = out
-        return carry
-
-    lax.fori_loop(lo, hi, one, 0)
+            carry[q] = carry[q] + out
+        return tuple(carry)
+
+    return lax.fori_loop(lo, hi, one, tuple(sums))
 
 
 def unpacking(land_ref, slot_row_ref, slot_lane_ref):
@@ -102,7 +103,7 @@
     fields[6] = wind * jnp.sin(angle_ref[...])
 
 
-def transport(trig_ref, spectrum_ref, land_ref, fields, base, ahead, behind, edges, lo, hi, beside):
+def transport(trig_ref, spectrum_ref, land_ref, fields, base, ahead, behind, edges, lo, hi):
     rows, lanes = iota((ROWS, COLS), 0), iota((ROWS, COLS), 1)
 
     def one(j, carry):
@@ -126,7 +127,6 @@
         base[j] = energy - change + wind
         ahead[j + 1] = ft
         behind[j] = bt
-        beside(j)
         return carry
 
     lax.fori_loop(lo, hi, one, 0)
@@ -163,16 +163,7 @@
             second = scaled * (energy * (c + d) - 2.0 * c * d)
             q_one[f * NDIR + j] = first
             q_two[f * NDIR + j] = second
-            n[(HALO + f) * NDIR + j] = -2.0 * (first + second)
-        return carry
-
-    lax.fori_loop(0, NDIR, one, 0)
-
-
-def decline(decay, square, x, n, z):
-    def one(j, carry):
-        for f in range(NY_DEV):
-            n[(HALO + f) * NDIR + j] -= (decay[f] * square) * x[z * PLANE_BINS + f * NDIR + j]
+            n[HALO + f, j] = -2.0 * (first + second)
         return carry
 
     lax.fori_loop(0, NDIR, one, 0)
@@ -186,7 +177,7 @@
                 at = j - turn
                 source[turn] = jnp.where(at < 0, at + NDIR, jnp.where(at >= NDIR, at - NDIR, at))
         for t in targets:
-            total = n[t * NDIR + j] if HALO <= t < HALO + NY_DEV else None
+            total = n[t, j] if HALO <= t < HALO + NY_DEV else None
             for row in range(4):
                 q = q_one if row < 2 else q_two
                 for step in range(2):
@@ -198,7 +189,7 @@
                         s = source[ROW_DIRS[row][which]]
                         term = mask_ref[at + s] * q[f * NDIR + s]
                         total = term if total is None else total + term
-            n[t * NDIR + j] = total
+            n[t, j] = total
         return carry
 
     lax.fori_loop(lo, hi, one, 0)
@@ -211,10 +202,10 @@
     const_ref, table_ref, coupling_ref,
     spectrum_ref, depth_ref, current_ref, slope_ref, forcing_ref, angle_ref, land_ref,
     fields, base, ahead, behind, edges, edge_in, slot_row, slot_lane, lane_ref, row_ref, ends_ref,
-    packed, x, n, q_one, q_two, up_in, down_in, source, sums, sums_in, mask_ref,
+    packed, x, n, q_one, q_two, up_in, down_in, source, sums, sums_in, column, decay, mask_ref,
     load_sem, part_sem,
     own_sem, send_y, recv_y, send_up, recv_up, send_down, recv_down, send_mean, recv_mean, send_edge, recv_edge,
-    send_cup, recv_cup, send_cdown, recv_cdown, send_back, recv_back,
+    send_cup, recv_cup, send_cdown, recv_cdown, send_back, recv_back, send_col, recv_col,
 ):
     space, spec = lax.axis_index("space"), lax.axis_index("spec")
     z, y = spec // NY_DEV, spec % NY_DEV
@@ -233,7 +224,7 @@
         pl.semaphore_signal(barrier, inc=1, device_id=device, device_id_type=pl.DeviceIdType.MESH)
 
     def spectrum_load(c):
-        part = pl.ds(c * PART, PART)
+        part = pl.ds(*IN_PARTS[c])
         return pltpu.make_async_copy(spectrum_hbm.at[part], spectrum_ref.at[part], part_sem.at[c])
 
     pairs = (
@@ -243,7 +234,7 @@
     )
     loads = [pltpu.make_async_copy(src, dst, load_sem.at[i]) for i, (src, dst) in enumerate(pairs)]
     loads[0].start()
-    for c in range(NCH):
+    for c in range(len(IN_PARTS)):
         spectrum_load(c).start()
     for load in loads[1:]:
         load.start()
@@ -275,7 +266,7 @@
             signal({"space": space + 1})
 
     def bins(freq, c):
-        return pl.ds(freq * NDIR + c * PART, PART)
+        return pl.ds(freq * NDIR + IN_PARTS[c][0], IN_PARTS[c][1])
 
     def eight(row):
         return pl.ds(pl.multiple_of(row * 8, 8), 8)
@@ -285,7 +276,7 @@
 
     def along_y(d, c):
         row = (y + d) % NY_DEV
-        src = packed.at[pl.ds(c * PART, PART), eight(row), :]
+        src = packed.at[pl.ds(*IN_PARTS[c]), eight(row), :]
         return remote(src, at(y, c), send_y.at[d, c], recv_y.at[y, c], to(z, row))
 
     def from_y(d, c):
@@ -310,56 +301,20 @@
             down(f, c, src).start()
 
     def own(c):
-        return pltpu.make_async_copy(packed.at[pl.ds(c * PART, PART), eight(y), :], at(y, c), own_sem.at[c])
+        return pltpu.make_async_copy(packed.at[pl.ds(*IN_PARTS[c]), eight(y), :], at(y, c), own_sem.at[c])
 
     loads[0].wait()
     packing(land_ref, lane_ref, row_ref, ends_ref)
-    for c in range(NCH):
+    mine = [jnp.zeros((8, COLS), F32)] * 4
+    for c, (first, number) in enumerate(IN_PARTS):
         spectrum_load(c).wait()
-        pack(spectrum_ref, lane_ref, row_ref, packed, c * PART, (c + 1) * PART)
+        mine = pack(spectrum_ref, lane_ref, row_ref, packed, first, first + number, mine)
         if c == 0:
             greet()
-        forward(y, c, packed.at[pl.ds(c * PART, PART), eight(y), :])
+        forward(y, c, packed.at[pl.ds(*IN_PARTS[c]), eight(y), :])
         for d in (1, 3, 2):
             along_y(d, c).start()
         own(c).start()
-
-    for load in loads[1:]:
-        load.wait()
-    transport_fields(
-        const_ref[2 * NDIR + spec], const_ref[2 * NDIR + NFREQ + spec],
-        depth_ref, current_ref, slope_ref, forcing_ref, angle_ref, fields,
-    )
-    for c in range(NCH):
-        for d in (1, 3, 2):
-            from_y(d, c).wait_recv()
-            forward((y + d) % NY_DEV, c)
-        transport(const_ref, spectrum_ref, land_ref, fields, base, ahead, behind, edges, c * PART, (c + 1) * PART,
-                  lambda j: quad_masks(table_ref, mask_ref, z, j))
-        own(c).wait()
-
-    def edge(side):
-        return remote(edges.at[side], edge_in.at[side], send_edge.at[side], recv_edge.at[side],
-                      {"space": space + 1 if side == 0 else space - 1})
-
-    @pl.when(even)
-    def _():
-        pl.semaphore_wait(barrier, in_space)
-
-    @pl.when(not_last)
-    def _():
-        edge(0).start()
-
-    @pl.when(not_first)
-    def _():
-        edge(1).start()
-
-    def add_up(k, total):
-        return total + x[z * PLANE_BINS + k]
-
-    total = lax.fori_loop(0, PLANE_BINS, add_up, jnp.zeros((8, COLS), F32), unroll=8)
-    sums[0, 0] = total
-    sums[1, 0] = total
 
     def across(stage, way):
         step = 1 << stage
@@ -392,54 +347,97 @@
             def _():
                 sums[way, stage + 1] = sums[way, stage]
 
+    for way in range(2):
+        for q in range(4):
+            sums[way, 0, 8 * q : 8 * q + 8, :] = mine[q]
     sums_out(0)
+    for load in loads[1:]:
+        load.wait()
+    transport_fields(
+        const_ref[2 * NDIR + spec], const_ref[2 * NDIR + NFREQ + spec],
+        depth_ref, current_ref, slope_ref, forcing_ref, angle_ref, fields,
+    )
+    for c, (first, number) in enumerate(IN_PARTS):
+        for d in (1, 3, 2):
+            from_y(d, c).wait_recv()
+            forward((y + d) % NY_DEV, c)
+        own(c).wait()
+        if c == len(IN_PARTS) - 1:
+            sums_come(0)
+            sums_out(1)
+        transport(const_ref, spectrum_ref, land_ref, fields, base, ahead, behind, edges, first, first + number)
+
+    def edge(side):
+        return remote(edges.at[side], edge_in.at[side], send_edge.at[side], recv_edge.at[side],
+                      {"space": space + 1 if side == 0 else space - 1})
+
+    @pl.when(even)
+    def _():
+        pl.semaphore_wait(barrier, in_space)
+
+    @pl.when(not_last)
+    def _():
+        edge(0).start()
+
+    @pl.when(not_first)
+    def _():
+        edge(1).start()
+
     ahead[0] = ahead[NDIR]
     behind[NDIR] = behind[0]
+
+    def masks(lo, hi):
+        def one(j, carry):
+            quad_masks(table_ref, mask_ref, z, j)
+            return carry
+
+        lax.fori_loop(lo, hi, one, 0)
+
+    masks(0, NDIR // 2)
+    sums_come(1)
+    sums_out(2)
+    masks(NDIR // 2, NDIR)
     unpacking(land_ref, slot_row, slot_lane)
-    sums_come(0)
-    sums_out(1)
 
     @pl.when(has_down)
     def _():
-        for c in range(NCH):
+        for c in range(len(IN_PARTS)):
             for f in range(1, NY_DEV):
                 remote(at(f - NY_DEV, c), at(f - NY_DEV, c), send_up.at[f - 1, c], recv_up.at[f - 1, c], to(z - 1, y)).wait_recv()
 
     @pl.when(has_up)
     def _():
-        for c in range(NCH):
+        for c in range(len(IN_PARTS)):
             for f in range(HALO):
                 remote(at(NY_DEV + f, c), at(NY_DEV + f, c), send_down.at[f, c], recv_down.at[f, c], to(z + 1, y)).wait_recv()
 
-    sums_come(1)
-    sums_out(2)
     quadruplets(table_ref, coupling_ref, x, q_one, q_two, n, z)
 
-    def give_up(f, c):
-        return remote(n.at[bins(HALO + NY_DEV + f, c)], up_in.at[bins(f, c)], send_cup.at[f, c], recv_cup.at[f, c], to(z + 1, y))
-
-    def give_down(f, c):
-        return remote(n.at[bins(f - 1, c)], down_in.at[bins(f - 1, c)], send_cdown.at[f - 1, c], recv_cdown.at[f - 1, c], to(z - 1, y))
-
-    for c in range(NCH):
-        scatter(mask_ref, q_one, q_two, n, (0, 1, 2, 7, 8, 9), c * PART, (c + 1) * PART)
+    def give_up(c):
+        part = pl.ds(*OUT_PARTS[c])
+        return remote(n.at[pl.ds(HALO + NY_DEV, HALO), part], up_in.at[:, part], send_cup.at[c], recv_cup.at[c], to(z + 1, y))
+
+    def give_down(c):
+        part = pl.ds(*OUT_PARTS[c])
+        return remote(n.at[pl.ds(0, HALO), part], down_in.at[:, part], send_cdown.at[c], recv_cdown.at[c], to(z - 1, y))
+
+    for c, (first, number) in enumerate(OUT_PARTS):
+        scatter(mask_ref, q_one, q_two, n, (0, 1, 2, 7, 8, 9), first, first + number)
 
         @pl.when(has_up)
         def _():
-            for f in range(HALO):
-                give_up(f, c).start()
+            give_up(c).start()
 
         @pl.when(has_down)
         def _():
-            for f in range(1, NY_DEV):
-                give_down(f, c).start()
+            give_down(c).start()
 
     scatter(mask_ref, q_one, q_two, n, (3, 4, 5, 6), 0, NDIR)
 
     @pl.when(z == 0)
     def _():
         def fold(j, carry):
-            n[HALO * NDIR + j] += n[j] + n[NDIR + j] + n[2 * NDIR + j]
+            n[HALO, j] += n[0, j] + n[1, j] + n[2, j]
             return carry
 
         lax.fori_loop(0, NDIR, fold, 0)
@@ -447,15 +445,19 @@
     @pl.when(z == PLANES - 1)
     def _():
         def fold(j, carry):
-            n[6 * NDIR + j] += n[7 * NDIR + j] + n[8 * NDIR + j] + n[9 * NDIR + j]
+            n[6, j] += n[7, j] + n[8, j] + n[9, j]
             return carry
 
         lax.fori_loop(0, NDIR, fold, 0)
 
     sums_come(2)
-    square = (sums[0, 3] + sums[1, 3] - sums[0, 0]) * (1.0 / (NFREQ * NDIR))
-    square = square * square
-    decline([const_ref[2 * NDIR + 2 * NFREQ + z * NY_DEV + f] for f in range(NY_DEV)], square, x, n, z)
+    column[y] = sums[0, 3] + sums[1, 3] - sums[0, 0]
+
+    def to_columns(d):
+        return remote(column.at[y], column.at[y], send_col.at[d], recv_col.at[y], to(z, (y + d) % NY_DEV))
+
+    for d in (2, 1, 3):
+        to_columns(d).start()
 
     for side, there in ((0, not_first), (1, not_last)):
         @pl.when(there)
@@ -469,7 +471,8 @@
 
     def back(d, c):
         f = (y + d) % NY_DEV
-        return remote(n.at[bins(HALO + f, c)], source.at[pl.ds(c * PART, PART), eight(y), :], send_back.at[d, c], recv_back.at[y, c], to(z, f))
+        part = pl.ds(*OUT_PARTS[c])
+        return remote(n.at[HALO + f, part], source.at[part, eight(y), :], send_back.at[d, c], recv_back.at[y, c], to(z, f))
 
     def finish(j, carry):
         base[j, 0:1, :] += edge_in[0, pl.ds(j, 1), :]
@@ -478,77 +481,88 @@
             rows = slice(8 * v, 8 * v + 8)
             added = unpack_block(lambda q: source[j, 8 * q : 8 * q + 8, :], slot_row[rows, :], slot_lane[rows, :], v)
             moved = base[j, rows, :] + ahead[j, rows, :] - behind[j + 1, rows, :]
+            moved = moved - decay[rows, :] * spectrum_ref[j, rows, :]
             out_ref[j, rows, :] = jnp.where(land_ref[rows, :] > 0, moved + added, 0.0)
         return carry
 
     def complete(c):
+        first, number = OUT_PARTS[c]
+        part = pl.ds(first, number)
+
         @pl.when(has_down)
         def _():
-            for f in range(HALO):
-                at_n = n.at[bins(HALO + NY_DEV + f, c)]
-                remote(at_n, up_in.at[bins(f, c)], send_cup.at[f, c], recv_cup.at[f, c], to(z - 1, y)).wait_recv()
+            remote(n.at[pl.ds(HALO + NY_DEV, HALO), part], up_in.at[:, part], send_cup.at[c], recv_cup.at[c], to(z - 1, y)).wait_recv()
 
             def add(j, carry):
                 for f in range(HALO):
-                    n[(HALO + f) * NDIR + j] += up_in[f * NDIR + j]
+                    n[HALO + f, j] += up_in[f, j]
                 return carry
 
-            lax.fori_loop(c * PART, (c + 1) * PART, add, 0)
+            lax.fori_loop(first, first + number, add, 0)
 
         @pl.when(has_up)
         def _():
-            for f in range(1, NY_DEV):
-                at_n = n.at[bins(f - 1, c)]
-                remote(at_n, down_in.at[bins(f - 1, c)], send_cdown.at[f - 1, c], recv_cdown.at[f - 1, c], to(z + 1, y)).wait_recv()
+            remote(n.at[pl.ds(0, HALO), part], down_in.at[:, part], send_cdown.at[c], recv_cdown.at[c], to(z + 1, y)).wait_recv()
 
             def add(j, carry):
                 for f in range(1, NY_DEV):
-                    n[(HALO + f) * NDIR + j] += down_in[(f - 1) * NDIR + j]
+                    n[HALO + f, j] += down_in[f - 1, j]
                 return carry
 
-            lax.fori_loop(c * PART, (c + 1) * PART, add, 0)
+            lax.fori_loop(first, first + number, add, 0)
 
         for d in (2, 1, 3):
             back(d, c).start()
 
         def keep(j, carry):
-            source[j, eight(y), :] = n[(HALO + y) * NDIR + j]
+            source[j, eight(y), :] = n[HALO + y, j]
             return carry
 
-        lax.fori_loop(c * PART, (c + 1) * PART, keep, 0)
+        lax.fori_loop(first, first + number, keep, 0)
 
     def conclude(c):
+        first, number = OUT_PARTS[c]
         for d in (1, 3, 2):
             f = (y + d) % NY_DEV
-            at_source = source.at[pl.ds(c * PART, PART), eight(f), :]
-            remote(n.at[bins(HALO, c)], at_source, send_back.at[d, c], recv_back.at[f, c], to(z, f)).wait_recv()
-        lax.fori_loop(c * PART, (c + 1) * PART, finish, 0)
-
-    for c in range(NCH):
+            at_source = source.at[pl.ds(first, number), eight(f), :]
+            remote(n.at[HALO, pl.ds(first, number)], at_source, send_back.at[d, c], recv_back.at[f, c], to(z, f)).wait_recv()
+        lax.fori_loop(first, first + number, finish, 0)
+
+    complete(0)
+    for d in (1, 3, 2):
+        f = (y + d) % NY_DEV
+        remote(column.at[f], column.at[f], send_col.at[d], recv_col.at[f], to(z, f)).wait_recv()
+    mean = (column[0] + column[1] + column[2] + column[3]) * (1.0 / (NFREQ * NDIR))
+    sums[0, 3] = mean * mean
+    rate = const_ref[2 * NDIR + 2 * NFREQ + spec]
+    for v in range(8):
+        rows = slice(8 * v, 8 * v + 8)
+        square = unpack_block(lambda q: sums[0, 3, 8 * q : 8 * q + 8, :], slot_row[rows, :], slot_lane[rows, :], v)
+        decay[rows, :] = rate * square
+    for c in range(1, len(OUT_PARTS)):
         complete(c)
-        if c:
-            conclude(c - 1)
-    conclude(NCH - 1)
-
-    for c in range(NCH):
+        conclude(c - 1)
+    conclude(len(OUT_PARTS) - 1)
+
+    for c in range(len(IN_PARTS)):
         for d in range(1, NY_DEV):
             along_y(d, c).wait_send()
 
     @pl.when(has_up)
     def _():
-        for c in range(NCH):
+        for c in range(len(IN_PARTS)):
             for f in range(1, NY_DEV):
                 up(f, c).wait_send()
-            for f in range(HALO):
-                give_up(f, c).wait_send()
+        for c in range(len(OUT_PARTS)):
+            give_up(c).wait_send()
 
     @pl.when(has_down)
     def _():
-        for c in range(NCH):
+        for c in range(len(IN_PARTS)):
             for f in range(HALO):
                 down(f, c).wait_send()
-            for f in range(1, NY_DEV):
-                give_down(f, c).wait_send()
+        for c in range(len(OUT_PARTS)):
+            give_down(c).wait_send()
 
     for stage in range(3):
         for way in range(2):
@@ -558,8 +572,9 @@
             def _():
                 copy.wait_send()
 
-    for c in range(NCH):
-        for d in range(1, NY_DEV):
+    for d in range(1, NY_DEV):
+        to_columns(d).wait_send()
+        for c in range(len(OUT_PARTS)):
             back(d, c).wait_send()
 
     @pl.when(not_last)
@@ -580,13 +595,13 @@
 
 def on_device(spectrum, sea_depth, current, depth_slope, wind_forcing, wind_angle, land_sea, quad_table, coupling):
     spectrum = spectrum.reshape(NDIR, ROWS, COLS)
-    dma = pltpu.SemaphoreType.DMA
+    dma, parts, backs = pltpu.SemaphoreType.DMA, len(IN_PARTS), len(OUT_PARTS)
     tile, field, two = pltpu.VMEM((ROWS, COLS), jnp.int32), pltpu.VMEM((ROWS, COLS), F32), pltpu.VMEM((2, ROWS, COLS), F32)
     longer = pltpu.VMEM((NDIR + 1, ROWS, COLS), F32)
     edges = pltpu.VMEM((2, NDIR, COLS), F32)
     own_bins = pltpu.VMEM((PLANE_BINS, 8, COLS), F32)
-    all_bins = pltpu.VMEM(((NY_DEV + 2 * HALO) * NDIR, 8, COLS), F32)
-    halo = pltpu.VMEM((HALO * NDIR, 8, COLS), F32)
+    all_bins = pltpu.VMEM((NY_DEV + 2 * HALO, NDIR, 8, COLS), F32)
+    halo = pltpu.VMEM((HALO, NDIR, 8, COLS), F32)
     packed = pltpu.VMEM((NDIR, PACKED, COLS), F32)
     out = pl.pallas_call(
         step_kernel,
@@ -599,14 +614,16 @@
             pltpu.VMEM((7, ROWS, COLS), F32), pltpu.VMEM((NDIR, ROWS, COLS), F32), longer, longer, edges, edges,
             tile, tile, tile, pltpu.VMEM((PACKED, COLS), jnp.int32), tile,
             packed, pltpu.VMEM((NFREQ * NDIR, 8, COLS), F32), all_bins, own_bins, own_bins, halo, halo, packed,
-            pltpu.VMEM((2, 4, 8, COLS), F32), pltpu.VMEM((2, 3, 8, COLS), F32), pltpu.SMEM((16 * PLANE_BINS,), F32),
-            dma((9,)), dma((NCH,)),
-            dma((NCH,)), dma((NY_DEV, NCH)), dma((NY_DEV, NCH)),
-            dma((HALO, NCH)), dma((HALO, NCH)), dma((HALO, NCH)), dma((HALO, NCH)),
+            pltpu.VMEM((2, 4, PACKED, COLS), F32), pltpu.VMEM((2, 3, PACKED, COLS), F32),
+            pltpu.VMEM((NY_DEV, PACKED, COLS), F32), field, pltpu.SMEM((16 * PLANE_BINS,), F32),
+            dma((9,)), dma((parts,)),
+            dma((parts,)), dma((NY_DEV, parts)), dma((NY_DEV, parts)),
+            dma((HALO, parts)), dma((HALO, parts)), dma((HALO, parts)), dma((HALO, parts)),
             dma((2, 3)), dma((2, 3)), dma((2,)), dma((2,)),
-            dma((HALO, NCH)), dma((HALO, NCH)), dma((HALO, NCH)), dma((HALO, NCH)), dma((NY_DEV, NCH)), dma((NY_DEV, NCH)),
+            dma((backs,)), dma((backs,)), dma((backs,)), dma((backs,)), dma((NY_DEV, backs)), dma((NY_DEV, backs)),
+            dma((NY_DEV,)), dma((NY_DEV,)),
         ],
-        compiler_params=pltpu.CompilerParams(vmem_limit_bytes=40 << 20, collective_id=0, has_side_effects=True),
+        compiler_params=pltpu.CompilerParams(vmem_limit_bytes=60 << 20, collective_id=0, has_side_effects=True),
     )(jnp.asarray(constants()), quad_table, coupling, spectrum, sea_depth, current, depth_slope, wind_forcing, wind_angle, land_sea)
     return out.reshape(1, NDIR, ROWS, COLS)
 

time: 59.1 us -> 48.7 us (0.82)
  the two profiles are of different devices: /device:TPU:6 before, /device:TPU:38 now
where the time goes in v3:
time: 48.7 us; the launch traced here: 48.6 us
  Pallas kernels  46.2 us (95%)
  local copies, waits for them, and re-layouts  2.41 us (5%)
    pallas_call x1, Pallas kernels, on_device(): pl.pallas_call(step_kernel, out_shape=jax.ShapeDtypeStruct((NDIR, ROWS, C...  46.2 us
    unnamed x1, local copies, waits for them, and re-layouts  2.41 us

profile of v3, /device:TPU:38, one launch (start us, length us, event | category | flops | bytes accessed | tf_op | source)
XLA Modules:
  0.0 48.6 jit_solution(16211286983439126009)
XLA Ops:
  0.0 46.2 %shard_map.100 = f32[36,64,128]{2,1,0:T(8,128)} custom-call(f32[168]{0:T(256)} %constant.2.clone.const_hbm, s32[4,1152]{1,0:T(4,128)} %table_hbm.1, f32[1152]{0:T(1024)} %coupling_hbm.1, f32[36,64,128]{2,1,0:T(8,128)} %bitcast.3, f32[64,128]{1,0:T(8,128)} %depth_hbm.1, f32[2,64,128]{2,1,0:T(8,128)} %current_hbm.1, f32[2,64,128]{2,1,0:T(8,128)} %slope_hbm.1, ...), custom_call_target="tpu_custom_call" | custom-call | tf_op jit(solution)/shard_map/pallas_call | solution.py:606
  46.2 2.4 %copy.12 = f32[1,36,64,128]{3,2,1,0:T(8,128)} copy(f32[1,36,64,128]{3,2,1,0:T(8,128)} %bitcast.2) | data formatting | bytes 2359296

commit v4 on v3

--- a/solution.py
+++ b/solution.py
@@ -132,23 +132,22 @@
     lax.fori_loop(lo, hi, one, 0)
 
 
-def quad_masks(table_ref, mask_ref, z, j):
-    def wrapped(turn):
-        at = j + turn
-        return jnp.where(at < 0, at + NDIR, jnp.where(at >= NDIR, at - NDIR, at))
-
-    for row in range(4):
-        turns = [wrapped(turn) for turn in ROW_DIRS[row]]
-        for f in range(NY_DEV):
-            freq = z * NY_DEV + f
-            near = jnp.clip(freq + 2 * ROW_SIGN[row], 0, NFREQ - 1)
-            far = jnp.clip(freq + 3 * ROW_SIGN[row], 0, NFREQ - 1)
-            far = jnp.where(far == near, -NFREQ, far)
-            bins = table_ref[row, z * PLANE_BINS + f * NDIR + j]
-            for step, target in enumerate((near, far)):
-                for which in range(2):
-                    at = ((row * 2 + step) * 2 + which) * PLANE_BINS + f * NDIR
-                    mask_ref[at + j] = jnp.where(bins == target * NDIR + turns[which], 1.0, 0.0).astype(F32)
+def quad_masks(table, mask_out):
+    shape = (4, NFREQ * NDIR)
+    row, k = iota(shape, 0), iota(shape, 1)
+    freq = (k * 1821) >> 16
+    direction = k - freq * NDIR
+    sign = 1 - 2 * (row & 1)
+    near = jnp.clip(freq + 2 * sign, 0, NFREQ - 1)
+    far = jnp.clip(freq + 3 * sign, 0, NFREQ - 1)
+    far = jnp.where(far == near, -NFREQ, far)
+    for which in range(2):
+        turn = jnp.where(row == 0, ROW_DIRS[0][which], ROW_DIRS[1][which])
+        turn = jnp.where(row == 2, ROW_DIRS[2][which], jnp.where(row == 3, ROW_DIRS[3][which], turn))
+        there = direction + turn
+        there = jnp.where(there < 0, there + NDIR, jnp.where(there >= NDIR, there - NDIR, there))
+        for step, target in enumerate((near, far)):
+            mask_out[step * 2 + which] = jnp.where(table == target * NDIR + there, 1.0, 0.0).astype(F32)
 
 
 def quadruplets(table_ref, coupling_ref, x, q_one, q_two, n, z):
@@ -169,7 +168,7 @@
     lax.fori_loop(0, NDIR, one, 0)
 
 
-def scatter(mask_ref, q_one, q_two, n, targets, lo, hi):
+def scatter(mask_ref, shift, q_one, q_two, n, targets, lo, hi):
     def one(j, carry):
         source = {}
         for turns in ROW_DIRS:
@@ -185,9 +184,8 @@
                     if not 0 <= f < NY_DEV:
                         continue
                     for which in range(2):
-                        at = ((row * 2 + step) * 2 + which) * PLANE_BINS + f * NDIR
                         s = source[ROW_DIRS[row][which]]
-                        term = mask_ref[at + s] * q[f * NDIR + s]
+                        term = mask_ref[step * 2 + which, row, shift + f * NDIR + s] * q[f * NDIR + s]
                         total = term if total is None else total + term
             n[t, j] = total
         return carry
@@ -198,12 +196,12 @@
 def step_kernel(
     const_hbm, table_hbm, coupling_hbm,
     spectrum_hbm, depth_hbm, current_hbm, slope_hbm, forcing_hbm, angle_hbm, land_hbm,
-    out_ref,
+    out_hbm,
     const_ref, table_ref, coupling_ref,
     spectrum_ref, depth_ref, current_ref, slope_ref, forcing_ref, angle_ref, land_ref,
     fields, base, ahead, behind, edges, edge_in, slot_row, slot_lane, lane_ref, row_ref, ends_ref,
-    packed, x, n, q_one, q_two, up_in, down_in, source, sums, sums_in, column, decay, mask_ref,
-    load_sem, part_sem,
+    packed, x, n, q_one, q_two, up_in, down_in, source, sums, sums_in, column, decay, table_v, mask_v, mask_ref,
+    load_sem, part_sem, mask_sem, out_sem,
     own_sem, send_y, recv_y, send_up, recv_up, send_down, recv_down, send_mean, recv_mean, send_edge, recv_edge,
     send_cup, recv_cup, send_cdown, recv_cdown, send_back, recv_back, send_col, recv_col,
 ):
@@ -230,7 +228,7 @@
     pairs = (
         (land_hbm, land_ref), (const_hbm, const_ref), (depth_hbm, depth_ref), (current_hbm, current_ref),
         (slope_hbm, slope_ref), (forcing_hbm, forcing_ref), (angle_hbm, angle_ref), (table_hbm, table_ref),
-        (coupling_hbm, coupling_ref),
+        (coupling_hbm, coupling_ref), (table_hbm, table_v),
     )
     loads = [pltpu.make_async_copy(src, dst, load_sem.at[i]) for i, (src, dst) in enumerate(pairs)]
     loads[0].start()
@@ -305,16 +303,27 @@
 
     loads[0].wait()
     packing(land_ref, lane_ref, row_ref, ends_ref)
-    mine = [jnp.zeros((8, COLS), F32)] * 4
-    for c, (first, number) in enumerate(IN_PARTS):
+    for c in range(len(IN_PARTS)):
         spectrum_load(c).wait()
-        mine = pack(spectrum_ref, lane_ref, row_ref, packed, first, first + number, mine)
-        if c == 0:
-            greet()
+    for load in loads[1:]:
+        load.wait()
+    odd = jnp.logical_not(even)
+
+    def send(c):
         forward(y, c, packed.at[pl.ds(*IN_PARTS[c]), eight(y), :])
         for d in (1, 3, 2):
             along_y(d, c).start()
         own(c).start()
+
+    mine = [jnp.zeros((8, COLS), F32)] * 4
+    for c, (first, number) in enumerate(IN_PARTS):
+        mine = pack(spectrum_ref, lane_ref, row_ref, packed, first, first + number, mine)
+        if c == 0:
+            greet()
+
+        @pl.when(even)
+        def _():
+            send(c)
 
     def across(stage, way):
         step = 1 << stage
@@ -351,21 +360,87 @@
         for q in range(4):
             sums[way, 0, 8 * q : 8 * q + 8, :] = mine[q]
     sums_out(0)
-    for load in loads[1:]:
-        load.wait()
-    transport_fields(
-        const_ref[2 * NDIR + spec], const_ref[2 * NDIR + NFREQ + spec],
-        depth_ref, current_ref, slope_ref, forcing_ref, angle_ref, fields,
-    )
-    for c, (first, number) in enumerate(IN_PARTS):
+    def move():
+        transport_fields(
+            const_ref[2 * NDIR + spec], const_ref[2 * NDIR + NFREQ + spec],
+            depth_ref, current_ref, slope_ref, forcing_ref, angle_ref, fields,
+        )
+        transport(const_ref, spectrum_ref, land_ref, fields, base, ahead, behind, edges, 0, NDIR)
+        ahead[0] = ahead[NDIR]
+        behind[NDIR] = behind[0]
+
+    @pl.when(odd)
+    def _():
+        move()
+        sums_come(0)
+        sums_out(1)
+        for c in range(len(IN_PARTS)):
+            send(c)
+
+    for c in range(len(IN_PARTS)):
         for d in (1, 3, 2):
             from_y(d, c).wait_recv()
             forward((y + d) % NY_DEV, c)
         own(c).wait()
-        if c == len(IN_PARTS) - 1:
-            sums_come(0)
-            sums_out(1)
-        transport(const_ref, spectrum_ref, land_ref, fields, base, ahead, behind, edges, first, first + number)
+
+    @pl.when(even)
+    def _():
+        sums_come(0)
+        sums_out(1)
+
+    @pl.when(odd)
+    def _():
+        sums_come(1)
+        sums_out(2)
+
+    quad_masks(table_v[...], mask_v)
+    shift = z * (PLANE_BINS - COLS)
+    masks = pltpu.make_async_copy(mask_v.at[:, :, pl.ds(pl.multiple_of(z * COLS, COLS), 2 * COLS)], mask_ref, mask_sem)
+    masks.start()
+    unpacking(land_ref, slot_row, slot_lane)
+
+    @pl.when(has_down)
+    def _():
+        for c in range(len(IN_PARTS)):
+            for f in range(1, NY_DEV):
+                remote(at(f - NY_DEV, c), at(f - NY_DEV, c), send_up.at[f - 1, c], recv_up.at[f - 1, c], to(z - 1, y)).wait_recv()
+
+    @pl.when(has_up)
+    def _():
+        for c in range(len(IN_PARTS)):
+            for f in range(HALO):
+                remote(at(NY_DEV + f, c), at(NY_DEV + f, c), send_down.at[f, c], recv_down.at[f, c], to(z + 1, y)).wait_recv()
+
+    quadruplets(table_ref, coupling_ref, x, q_one, q_two, n, z)
+    masks.wait()
+
+    @pl.when(even)
+    def _():
+        sums_come(1)
+        sums_out(2)
+
+    def give_up(c):
+        part = pl.ds(*OUT_PARTS[c])
+        return remote(n.at[pl.ds(HALO + NY_DEV, HALO), part], up_in.at[:, part], send_cup.at[c], recv_cup.at[c], to(z + 1, y))
+
+    def give_down(c):
+        part = pl.ds(*OUT_PARTS[c])
+        return remote(n.at[pl.ds(0, HALO), part], down_in.at[:, part], send_cdown.at[c], recv_cdown.at[c], to(z - 1, y))
+
+    for c, (first, number) in enumerate(OUT_PARTS):
+        scatter(mask_ref, shift, q_one, q_two, n, (0, 1, 2, 7, 8, 9), first, first + number)
+
+        @pl.when(has_up)
+        def _():
+            give_up(c).start()
+
+        @pl.when(has_down)
+        def _():
+            give_down(c).start()
+
+    @pl.when(even)
+    def _():
+        move()
 
     def edge(side):
         return remote(edges.at[side], edge_in.at[side], send_edge.at[side], recv_edge.at[side],
@@ -383,56 +458,7 @@
     def _():
         edge(1).start()
 
-    ahead[0] = ahead[NDIR]
-    behind[NDIR] = behind[0]
-
-    def masks(lo, hi):
-        def one(j, carry):
-            quad_masks(table_ref, mask_ref, z, j)
-            return carry
-
-        lax.fori_loop(lo, hi, one, 0)
-
-    masks(0, NDIR // 2)
-    sums_come(1)
-    sums_out(2)
-    masks(NDIR // 2, NDIR)
-    unpacking(land_ref, slot_row, slot_lane)
-
-    @pl.when(has_down)
-    def _():
-        for c in range(len(IN_PARTS)):
-            for f in range(1, NY_DEV):
-                remote(at(f - NY_DEV, c), at(f - NY_DEV, c), send_up.at[f - 1, c], recv_up.at[f - 1, c], to(z - 1, y)).wait_recv()
-
-    @pl.when(has_up)
-    def _():
-        for c in range(len(IN_PARTS)):
-            for f in range(HALO):
-                remote(at(NY_DEV + f, c), at(NY_DEV + f, c), send_down.at[f, c], recv_down.at[f, c], to(z + 1, y)).wait_recv()
-
-    quadruplets(table_ref, coupling_ref, x, q_one, q_two, n, z)
-
-    def give_up(c):
-        part = pl.ds(*OUT_PARTS[c])
-        return remote(n.at[pl.ds(HALO + NY_DEV, HALO), part], up_in.at[:, part], send_cup.at[c], recv_cup.at[c], to(z + 1, y))
-
-    def give_down(c):
-        part = pl.ds(*OUT_PARTS[c])
-        return remote(n.at[pl.ds(0, HALO), part], down_in.at[:, part], send_cdown.at[c], recv_cdown.at[c], to(z - 1, y))
-
-    for c, (first, number) in enumerate(OUT_PARTS):
-        scatter(mask_ref, q_one, q_two, n, (0, 1, 2, 7, 8, 9), first, first + number)
-
-        @pl.when(has_up)
-        def _():
-            give_up(c).start()
-
-        @pl.when(has_down)
-        def _():
-            give_down(c).start()
-
-    scatter(mask_ref, q_one, q_two, n, (3, 4, 5, 6), 0, NDIR)
+    scatter(mask_ref, shift, q_one, q_two, n, (3, 4, 5, 6), 0, NDIR)
 
     @pl.when(z == 0)
     def _():
@@ -449,15 +475,6 @@
             return carry
 
         lax.fori_loop(0, NDIR, fold, 0)
-
-    sums_come(2)
-    column[y] = sums[0, 3] + sums[1, 3] - sums[0, 0]
-
-    def to_columns(d):
-        return remote(column.at[y], column.at[y], send_col.at[d], recv_col.at[y], to(z, (y + d) % NY_DEV))
-
-    for d in (2, 1, 3):
-        to_columns(d).start()
 
     for side, there in ((0, not_first), (1, not_last)):
         @pl.when(there)
@@ -482,7 +499,7 @@
             added = unpack_block(lambda q: source[j, 8 * q : 8 * q + 8, :], slot_row[rows, :], slot_lane[rows, :], v)
             moved = base[j, rows, :] + ahead[j, rows, :] - behind[j + 1, rows, :]
             moved = moved - decay[rows, :] * spectrum_ref[j, rows, :]
-            out_ref[j, rows, :] = jnp.where(land_ref[rows, :] > 0, moved + added, 0.0)
+            base[j, rows, :] = jnp.where(land_ref[rows, :] > 0, moved + added, 0.0)
         return carry
 
     def complete(c):
@@ -519,6 +536,10 @@
             return carry
 
         lax.fori_loop(first, first + number, keep, 0)
+
+    def result(c):
+        part = pl.ds(*OUT_PARTS[c])
+        return pltpu.make_async_copy(base.at[part], out_hbm.at[part], out_sem.at[c])
 
     def conclude(c):
         first, number = OUT_PARTS[c]
@@ -527,8 +548,19 @@
             at_source = source.at[pl.ds(first, number), eight(f), :]
             remote(n.at[HALO, pl.ds(first, number)], at_source, send_back.at[d, c], recv_back.at[f, c], to(z, f)).wait_recv()
         lax.fori_loop(first, first + number, finish, 0)
+        result(c).start()
 
     complete(0)
+    sums_come(2)
+    column[y] = sums[0, 3] + sums[1, 3] - sums[0, 0]
+
+    def to_columns(d):
+        return remote(column.at[y], column.at[y], send_col.at[d], recv_col.at[y], to(z, (y + d) % NY_DEV))
+
+    for d in (2, 1, 3):
+        to_columns(d).start()
+
+    complete(1)
     for d in (1, 3, 2):
         f = (y + d) % NY_DEV
         remote(column.at[f], column.at[f], send_col.at[d], recv_col.at[f], to(z, f)).wait_recv()
@@ -539,7 +571,8 @@
         rows = slice(8 * v, 8 * v + 8)
         square = unpack_block(lambda q: sums[0, 3, 8 * q : 8 * q + 8, :], slot_row[rows, :], slot_lane[rows, :], v)
         decay[rows, :] = rate * square
-    for c in range(1, len(OUT_PARTS)):
+    conclude(0)
+    for c in range(2, len(OUT_PARTS)):
         complete(c)
         conclude(c - 1)
     conclude(len(OUT_PARTS) - 1)
@@ -576,6 +609,8 @@
         to_columns(d).wait_send()
         for c in range(len(OUT_PARTS)):
             back(d, c).wait_send()
+    for c in range(len(OUT_PARTS)):
+        result(c).wait()
 
     @pl.when(not_last)
     def _():
@@ -607,7 +642,7 @@
         step_kernel,
         out_shape=jax.ShapeDtypeStruct((NDIR, ROWS, COLS), F32),
         in_specs=[pl.BlockSpec(memory_space=pltpu.HBM)] * 10,
-        out_specs=VMEM,
+        out_specs=pl.BlockSpec(memory_space=pltpu.HBM),
         scratch_shapes=[
             pltpu.SMEM((2 * NDIR + 3 * NFREQ,), F32), pltpu.SMEM((4, NFREQ * NDIR), jnp.int32), pltpu.SMEM((NFREQ * NDIR,), F32),
             pltpu.VMEM((NDIR, ROWS, COLS), F32), field, two, two, field, field, tile,
@@ -615,8 +650,9 @@
             tile, tile, tile, pltpu.VMEM((PACKED, COLS), jnp.int32), tile,
             packed, pltpu.VMEM((NFREQ * NDIR, 8, COLS), F32), all_bins, own_bins, own_bins, halo, halo, packed,
             pltpu.VMEM((2, 4, PACKED, COLS), F32), pltpu.VMEM((2, 3, PACKED, COLS), F32),
-            pltpu.VMEM((NY_DEV, PACKED, COLS), F32), field, pltpu.SMEM((16 * PLANE_BINS,), F32),
-            dma((9,)), dma((parts,)),
+            pltpu.VMEM((NY_DEV, PACKED, COLS), F32), field,
+            pltpu.VMEM((4, NFREQ * NDIR), jnp.int32), pltpu.VMEM((4, 4, NFREQ * NDIR), F32), pltpu.SMEM((4, 4, 2 * COLS), F32),
+            dma((10,)), dma((parts,)), dma, dma((backs,)),
             dma((parts,)), dma((NY_DEV, parts)), dma((NY_DEV, parts)),
             dma((HALO, parts)), dma((HALO, parts)), dma((HALO, parts)), dma((HALO, parts)),
             dma((2, 3)), dma((2, 3)), dma((2,)), dma((2,)),

time: 48.7 us -> 47 us (0.965)
  the two profiles are of different devices: /device:TPU:38 before, /device:TPU:100 now
where the time goes in v4:
time: 47 us; the launch traced here: 46.9 us
  Pallas kernels  44.5 us (95%)
  local copies, waits for them, and re-layouts  2.41 us (5%)
    pallas_call x1, Pallas kernels, on_device(): pl.pallas_call(step_kernel, out_shape=jax.ShapeDtypeStruct((NDIR, ROWS, C...  44.5 us
    unnamed x1, local copies, waits for them, and re-layouts  2.41 us

profile of v4, /device:TPU:100, one launch (start us, length us, event | category | flops | bytes accessed | tf_op | source)
XLA Modules:
  0.0 46.9 jit_solution(10152752497718255095)
XLA Ops:
  0.0 44.5 %shard_map.100 = f32[36,64,128]{2,1,0:T(8,128)} custom-call(f32[168]{0:T(256)} %constant.2.clone.const_hbm, s32[4,1152]{1,0:T(4,128)} %table_hbm.1, f32[1152]{0:T(1024)} %coupling_hbm.1, f32[36,64,128]{2,1,0:T(8,128)} %bitcast.3, f32[64,128]{1,0:T(8,128)} %depth_hbm.1, f32[2,64,128]{2,1,0:T(8,128)} %current_hbm.1, f32[2,64,128]{2,1,0:T(8,128)} %slope_hbm.1, ...), custom_call_target="tpu_custom_call" | custom-call | tf_op jit(solution)/shard_map/pallas_call | solution.py:641
  44.5 2.4 %copy.12 = f32[1,36,64,128]{3,2,1,0:T(8,128)} copy(f32[1,36,64,128]{3,2,1,0:T(8,128)} %bitcast.2) | data formatting | bytes 2359296

commit v5 on v4

--- a/solution.py
+++ b/solution.py
@@ -11,8 +11,8 @@
 PACKED = 32
 PLANES = NFREQ // NY_DEV
 HALO = 3
-IN_PARTS = ((0, 6), (6, 12), (18, 18))
-OUT_PARTS = ((0, 16), (16, 14), (30, 6))
+IN_PARTS = ((0, 12), (12, 12), (24, 12))
+OUT_PARTS = ((0, 18), (18, 18))
 PLANE_BINS = NY_DEV * NDIR
 F32 = jnp.float32
 VMEM = pl.BlockSpec(memory_space=pltpu.VMEM)
@@ -72,7 +72,7 @@
             carry[q] = carry[q] + out
         return tuple(carry)
 
-    return lax.fori_loop(lo, hi, one, tuple(sums))
+    return lax.fori_loop(lo, hi, one, tuple(sums), unroll=6)
 
 
 def unpacking(land_ref, slot_row_ref, slot_lane_ref):
@@ -129,7 +129,7 @@
         behind[j] = bt
         return carry
 
-    lax.fori_loop(lo, hi, one, 0)
+    lax.fori_loop(lo, hi, one, 0, unroll=4)
 
 
 def quad_masks(table, mask_out):
@@ -165,7 +165,7 @@
             n[HALO + f, j] = -2.0 * (first + second)
         return carry
 
-    lax.fori_loop(0, NDIR, one, 0)
+    lax.fori_loop(0, NDIR, one, 0, unroll=4)
 
 
 def scatter(mask_ref, shift, q_one, q_two, n, targets, lo, hi):
@@ -190,7 +190,7 @@
             n[t, j] = total
         return carry
 
-    lax.fori_loop(lo, hi, one, 0)
+    lax.fori_loop(lo, hi, one, 0, unroll=3)
 
 
 def step_kernel(
@@ -238,7 +238,8 @@
         load.start()
 
     barrier = pltpu.get_barrier_semaphore()
-    even = space % 2 == 0
+    leads = space % 2 == 1
+    follows = jnp.logical_not(leads)
     in_spec = NY_DEV - 1 + has_up.astype(jnp.int32) + has_down.astype(jnp.int32)
     in_space = not_first.astype(jnp.int32) + not_last.astype(jnp.int32)
     for d in range(1, NY_DEV):
@@ -253,7 +254,7 @@
         signal(to(z - 1, y))
 
     def greet():
-        pl.semaphore_wait(barrier, in_spec + jnp.where(even, 0, in_space))
+        pl.semaphore_wait(barrier, in_spec + jnp.where(leads, 0, in_space))
 
         @pl.when(not_first)
         def _():
@@ -307,7 +308,6 @@
         spectrum_load(c).wait()
     for load in loads[1:]:
         load.wait()
-    odd = jnp.logical_not(even)
 
     def send(c):
         forward(y, c, packed.at[pl.ds(*IN_PARTS[c]), eight(y), :])
@@ -321,7 +321,7 @@
         if c == 0:
             greet()
 
-        @pl.when(even)
+        @pl.when(leads)
         def _():
             send(c)
 
@@ -369,7 +369,7 @@
         ahead[0] = ahead[NDIR]
         behind[NDIR] = behind[0]
 
-    @pl.when(odd)
+    @pl.when(follows)
     def _():
         move()
         sums_come(0)
@@ -383,12 +383,12 @@
             forward((y + d) % NY_DEV, c)
         own(c).wait()
 
-    @pl.when(even)
+    @pl.when(leads)
     def _():
         sums_come(0)
         sums_out(1)
 
-    @pl.when(odd)
+    @pl.when(follows)
     def _():
         sums_come(1)
         sums_out(2)
@@ -414,7 +414,7 @@
     quadruplets(table_ref, coupling_ref, x, q_one, q_two, n, z)
     masks.wait()
 
-    @pl.when(even)
+    @pl.when(leads)
     def _():
         sums_come(1)
         sums_out(2)
@@ -438,7 +438,7 @@
         def _():
             give_down(c).start()
 
-    @pl.when(even)
+    @pl.when(leads)
     def _():
         move()
 
@@ -446,7 +446,7 @@
         return remote(edges.at[side], edge_in.at[side], send_edge.at[side], recv_edge.at[side],
                       {"space": space + 1 if side == 0 else space - 1})
 
-    @pl.when(even)
+    @pl.when(leads)
     def _():
         pl.semaphore_wait(barrier, in_space)
 
@@ -515,7 +515,7 @@
                     n[HALO + f, j] += up_in[f, j]
                 return carry
 
-            lax.fori_loop(first, first + number, add, 0)
+            lax.fori_loop(first, first + number, add, 0, unroll=2)
 
         @pl.when(has_up)
         def _():
@@ -526,7 +526,7 @@
                     n[HALO + f, j] += down_in[f - 1, j]
                 return carry
 
-            lax.fori_loop(first, first + number, add, 0)
+            lax.fori_loop(first, first + number, add, 0, unroll=2)
 
         for d in (2, 1, 3):
             back(d, c).start()
@@ -535,7 +535,7 @@
             source[j, eight(y), :] = n[HALO + y, j]
             return carry
 
-        lax.fori_loop(first, first + number, keep, 0)
+        lax.fori_loop(first, first + number, keep, 0, unroll=2)
 
     def result(c):
         part = pl.ds(*OUT_PARTS[c])
@@ -547,7 +547,7 @@
             f = (y + d) % NY_DEV
             at_source = source.at[pl.ds(first, number), eight(f), :]
             remote(n.at[HALO, pl.ds(first, number)], at_source, send_back.at[d, c], recv_back.at[f, c], to(z, f)).wait_recv()
-        lax.fori_loop(first, first + number, finish, 0)
+        lax.fori_loop(first, first + number, finish, 0, unroll=6)
         result(c).start()
 
     complete(0)

time: 47 us -> 43 us (0.915)
  the two profiles are of different devices: /device:TPU:100 before, /device:TPU:66 now
where the time goes in v5:
time: 43 us; the launch traced here: 42.9 us
  Pallas kernels  40.4 us (94%)
  local copies, waits for them, and re-layouts  2.41 us (6%)
    pallas_call x1, Pallas kernels, on_device(): pl.pallas_call(step_kernel, out_shape=jax.ShapeDtypeStruct((NDIR, ROWS, C...  40.4 us
    unnamed x1, local copies, waits for them, and re-layouts  2.41 us

profile of v5, /device:TPU:66, one launch (start us, length us, event | category | flops | bytes accessed | tf_op | source)
XLA Modules:
  0.0 42.9 jit_solution(7445372888367338808)
XLA Ops:
  0.0 40.4 %shard_map.100 = f32[36,64,128]{2,1,0:T(8,128)} custom-call(f32[168]{0:T(256)} %constant.2.clone.const_hbm, s32[4,1152]{1,0:T(4,128)} %table_hbm.1, f32[1152]{0:T(1024)} %coupling_hbm.1, f32[36,64,128]{2,1,0:T(8,128)} %bitcast.3, f32[64,128]{1,0:T(8,128)} %depth_hbm.1, f32[2,64,128]{2,1,0:T(8,128)} %current_hbm.1, f32[2,64,128]{2,1,0:T(8,128)} %slope_hbm.1, ...), custom_call_target="tpu_custom_call" | custom-call | tf_op jit(solution)/shard_map/pallas_call | solution.py:641
  40.4 2.4 %copy.12 = f32[1,36,64,128]{3,2,1,0:T(8,128)} copy(f32[1,36,64,128]{3,2,1,0:T(8,128)} %bitcast.2) | data formatting | bytes 2359296

commit v6 on v5

--- a/solution.py
+++ b/solution.py
@@ -12,7 +12,7 @@
 PLANES = NFREQ // NY_DEV
 HALO = 3
 IN_PARTS = ((0, 12), (12, 12), (24, 12))
-OUT_PARTS = ((0, 18), (18, 18))
+OUT_PARTS = ((0, 24), (24, 12))
 PLANE_BINS = NY_DEV * NDIR
 F32 = jnp.float32
 VMEM = pl.BlockSpec(memory_space=pltpu.VMEM)
@@ -372,8 +372,6 @@
     @pl.when(follows)
     def _():
         move()
-        sums_come(0)
-        sums_out(1)
         for c in range(len(IN_PARTS)):
             send(c)
 
@@ -382,16 +380,10 @@
             from_y(d, c).wait_recv()
             forward((y + d) % NY_DEV, c)
         own(c).wait()
-
-    @pl.when(leads)
-    def _():
-        sums_come(0)
-        sums_out(1)
-
-    @pl.when(follows)
-    def _():
-        sums_come(1)
-        sums_out(2)
+        if c == 1:
+            sums_come(0)
+            sums_out(1)
+
 
     quad_masks(table_v[...], mask_v)
     shift = z * (PLANE_BINS - COLS)
@@ -413,11 +405,8 @@
 
     quadruplets(table_ref, coupling_ref, x, q_one, q_two, n, z)
     masks.wait()
-
-    @pl.when(leads)
-    def _():
-        sums_come(1)
-        sums_out(2)
+    sums_come(1)
+    sums_out(2)
 
     def give_up(c):
         part = pl.ds(*OUT_PARTS[c])

time: 43 us -> 41.5 us (0.965)
  Pallas kernels: 40.4 us -> 38.9 us
    pallas_call x1, Pallas kernels: 40.4 us -> 38.9 us  [on_device(): pl.pallas_call(step_kernel, out_shape=jax.ShapeDtypeStruct((NDIR, ROWS, C...]
where the time goes in v6:
time: 41.5 us; the launch traced here: 41.4 us
  Pallas kernels  38.9 us (94%)
  local copies, waits for them, and re-layouts  2.41 us (6%)
    pallas_call x1, Pallas kernels, on_device(): pl.pallas_call(step_kernel, out_shape=jax.ShapeDtypeStruct((NDIR, ROWS, C...  38.9 us
    unnamed x1, local copies, waits for them, and re-layouts  2.41 us

profile of v6, /device:TPU:66, one launch (start us, length us, event | category | flops | bytes accessed | tf_op | source)
XLA Modules:
  0.0 41.4 jit_solution(16710004901257138640)
XLA Ops:
  0.0 38.9 %shard_map.100 = f32[36,64,128]{2,1,0:T(8,128)} custom-call(f32[168]{0:T(256)} %constant.2.clone.const_hbm, s32[4,1152]{1,0:T(4,128)} %table_hbm.1, f32[1152]{0:T(1024)} %coupling_hbm.1, f32[36,64,128]{2,1,0:T(8,128)} %bitcast.3, f32[64,128]{1,0:T(8,128)} %depth_hbm.1, f32[2,64,128]{2,1,0:T(8,128)} %current_hbm.1, f32[2,64,128]{2,1,0:T(8,128)} %slope_hbm.1, ...), custom_call_target="tpu_custom_call" | custom-call | tf_op jit(solution)/shard_map/pallas_call | solution.py:630
  38.9 2.4 %copy.12 = f32[1,36,64,128]{3,2,1,0:T(8,128)} copy(f32[1,36,64,128]{3,2,1,0:T(8,128)} %bitcast.2) | data formatting | bytes 2359296

commit v7 on v6

--- a/solution.py
+++ b/solution.py
@@ -304,10 +304,6 @@
 
     loads[0].wait()
     packing(land_ref, lane_ref, row_ref, ends_ref)
-    for c in range(len(IN_PARTS)):
-        spectrum_load(c).wait()
-    for load in loads[1:]:
-        load.wait()
 
     def send(c):
         forward(y, c, packed.at[pl.ds(*IN_PARTS[c]), eight(y), :])
@@ -317,6 +313,7 @@
 
     mine = [jnp.zeros((8, COLS), F32)] * 4
     for c, (first, number) in enumerate(IN_PARTS):
+        spectrum_load(c).wait()
         mine = pack(spectrum_ref, lane_ref, row_ref, packed, first, first + number, mine)
         if c == 0:
             greet()
@@ -324,6 +321,9 @@
         @pl.when(leads)
         def _():
             send(c)
+
+    for load in loads[1:]:
+        load.wait()
 
     def across(stage, way):
         step = 1 << stage
@@ -380,11 +380,10 @@
             from_y(d, c).wait_recv()
             forward((y + d) % NY_DEV, c)
         own(c).wait()
-        if c == 1:
-            sums_come(0)
-            sums_out(1)
-
-
+
+
+    sums_come(0)
+    sums_out(1)
     quad_masks(table_v[...], mask_v)
     shift = z * (PLANE_BINS - COLS)
     masks = pltpu.make_async_copy(mask_v.at[:, :, pl.ds(pl.multiple_of(z * COLS, COLS), 2 * COLS)], mask_ref, mask_sem)
@@ -405,8 +404,11 @@
 
     quadruplets(table_ref, coupling_ref, x, q_one, q_two, n, z)
     masks.wait()
-    sums_come(1)
-    sums_out(2)
+
+    @pl.when(follows)
+    def _():
+        sums_come(1)
+        sums_out(2)
 
     def give_up(c):
         part = pl.ds(*OUT_PARTS[c])
@@ -429,6 +431,8 @@
 
     @pl.when(leads)
     def _():
+        sums_come(1)
+        sums_out(2)
         move()
 
     def edge(side):

time: 41.5 us -> 41.6 us (level); the launches traced: 41.4 us -> 40.9 us
    pallas_call x1, Pallas kernels: 38.9 us -> 38.5 us  [on_device(): pl.pallas_call(step_kernel, out_shape=jax.ShapeDtypeStruct((NDIR, ROWS, C...]
where the time goes in v7:
time: 41.6 us; the launch traced here: 40.9 us
  Pallas kernels  38.5 us (93%)
  local copies, waits for them, and re-layouts  2.41 us (6%)
    pallas_call x1, Pallas kernels, on_device(): pl.pallas_call(step_kernel, out_shape=jax.ShapeDtypeStruct((NDIR, ROWS, C...  38.5 us
    unnamed x1, local copies, waits for them, and re-layouts  2.41 us

profile of v7, /device:TPU:66, one launch (start us, length us, event | category | flops | bytes accessed | tf_op | source)
XLA Modules:
  0.0 40.9 jit_solution(13945382996211375655)
XLA Ops:
  0.0 38.5 %shard_map.100 = f32[36,64,128]{2,1,0:T(8,128)} custom-call(f32[168]{0:T(256)} %constant.2.clone.const_hbm, s32[4,1152]{1,0:T(4,128)} %table_hbm.1, f32[1152]{0:T(1024)} %coupling_hbm.1, f32[36,64,128]{2,1,0:T(8,128)} %bitcast.3, f32[64,128]{1,0:T(8,128)} %depth_hbm.1, f32[2,64,128]{2,1,0:T(8,128)} %current_hbm.1, f32[2,64,128]{2,1,0:T(8,128)} %slope_hbm.1, ...), custom_call_target="tpu_custom_call" | custom-call | tf_op jit(solution)/shard_map/pallas_call | solution.py:634
  38.5 2.4 %copy.12 = f32[1,36,64,128]{3,2,1,0:T(8,128)} copy(f32[1,36,64,128]{3,2,1,0:T(8,128)} %bitcast.2) | data formatting | bytes 2359296

commit v8 on v6

--- a/solution.py
+++ b/solution.py
@@ -304,10 +304,6 @@
 
     loads[0].wait()
     packing(land_ref, lane_ref, row_ref, ends_ref)
-    for c in range(len(IN_PARTS)):
-        spectrum_load(c).wait()
-    for load in loads[1:]:
-        load.wait()
 
     def send(c):
         forward(y, c, packed.at[pl.ds(*IN_PARTS[c]), eight(y), :])
@@ -317,6 +313,7 @@
 
     mine = [jnp.zeros((8, COLS), F32)] * 4
     for c, (first, number) in enumerate(IN_PARTS):
+        spectrum_load(c).wait()
         mine = pack(spectrum_ref, lane_ref, row_ref, packed, first, first + number, mine)
         if c == 0:
             greet()
@@ -324,6 +321,9 @@
         @pl.when(leads)
         def _():
             send(c)
+
+    for load in loads[1:]:
+        load.wait()
 
     def across(stage, way):
         step = 1 << stage

time: 41.5 us -> 41.5 us (level)
  no operation moved by 1% of the time
where the time goes in v8:
time: 41.5 us; the launch traced here: 41.4 us
  Pallas kernels  38.9 us (94%)
  local copies, waits for them, and re-layouts  2.41 us (6%)
    pallas_call x1, Pallas kernels, on_device(): pl.pallas_call(step_kernel, out_shape=jax.ShapeDtypeStruct((NDIR, ROWS, C...  38.9 us
    unnamed x1, local copies, waits for them, and re-layouts  2.41 us

profile of v8, /device:TPU:66, one launch (start us, length us, event | category | flops | bytes accessed | tf_op | source)
XLA Modules:
  0.0 41.4 jit_solution(6952260645963193078)
XLA Ops:
  0.0 38.9 %shard_map.100 = f32[36,64,128]{2,1,0:T(8,128)} custom-call(f32[168]{0:T(256)} %constant.2.clone.const_hbm, s32[4,1152]{1,0:T(4,128)} %table_hbm.1, f32[1152]{0:T(1024)} %coupling_hbm.1, f32[36,64,128]{2,1,0:T(8,128)} %bitcast.3, f32[64,128]{1,0:T(8,128)} %depth_hbm.1, f32[2,64,128]{2,1,0:T(8,128)} %current_hbm.1, f32[2,64,128]{2,1,0:T(8,128)} %slope_hbm.1, ...), custom_call_target="tpu_custom_call" | custom-call | tf_op jit(solution)/shard_map/pallas_call | solution.py:630
  38.9 2.4 %copy.12 = f32[1,36,64,128]{3,2,1,0:T(8,128)} copy(f32[1,36,64,128]{3,2,1,0:T(8,128)} %bitcast.2) | data formatting | bytes 2359296
